TPU v7x, 128 devices: a whole 4x4x4 slice. The times are simulated.
128 devices in a mesh: seq: 16 (over z_hi, x, core), head: 8 (over y, z_lo).
Axes of the slice: x: 4, y: 4, z: 4 (z_hi: 2, z_lo: 2; z = z_hi * 2 + z_lo), core: 2. Of those that a mesh axis runs over, the one named last changes fastest.
Arguments:
- hidden: bfloat16 [16384, 2048], P(('seq', 'head')), may hold values from -41 to 41
- w_qkv: bfloat16 [2048, 3072], replicated, may hold values from -0.125 to 0.125
- w_out: bfloat16 [2048, 2048], replicated, may hold values from -0.125 to 0.125
- seg_ids: int32 [16384], replicated, may hold values from 0 to 7, never falling along the last dimension, each value on 1 to 8192 neighbouring positions
- live: int32 [16384], replicated, may hold values 0 or 1
- page_table: int32 [1024], replicated, may hold values from 0 to 1023, as said below
Outputs:
- mixed: bfloat16 [16384, 2048], P(('seq', 'head'))
- kv_pool: bfloat16 [8, 1024, 16, 128], P('head', 'seq')
Inputs may be any that keep to these rules, and one draw needn't show every extreme that they name: `page_table`: A permutation of the 1024 pages; pool shard r along seq holds pages r * 64 to (r + 1) * 64 - 1, and the 64 logical pages of each seq group go exactly 4 to each pool shard.
All inputs are finite; a program needn't handle non-finite values.
Results may differ from a plain program's by a relative error of at most 0.0059.
The roundings to bfloat16 on the way count: a program that leaves them out, or rounds other values in their place, can miss the bound.
Values may be sent and summed in bfloat16 or wider, within the bound.
A program may use at most 128 MiB of HBM per device.

v0:
```python
import math

import jax
import jax.numpy as jnp
from jax import lax
from jax.sharding import PartitionSpec as P

KVH = 8
HD = 64
PAGE = 16
QPK = 4


def shards(hidden, w_qkv, w_out, seg_ids, live, page_table):
    heads_n = lax.axis_size("head")
    head_at = lax.axis_index("head")
    seq_at = lax.axis_index("seq")
    groups_here = KVH // heads_n
    per_group = (QPK + 2) * HD
    columns = groups_here * per_group
    w_here = lax.dynamic_slice_in_dim(w_qkv, head_at * columns, columns, 1)
    grouped = jnp.dot(
        lax.all_gather(hidden, "head", axis=0, tiled=True),
        w_here,
        preferred_element_type=jnp.float32,
    ).astype(jnp.bfloat16)
    group_rows = grouped.shape[0]
    shaped = grouped.reshape(group_rows, groups_here, QPK + 2, HD)
    queries = shaped[:, :, :QPK]
    keyvals = shaped[:, :, QPK:].reshape(group_rows, groups_here, 2 * HD)
    first_row = seq_at * group_rows
    q_index = first_row + jnp.arange(group_rows, dtype=jnp.int32)
    q_seg = lax.dynamic_slice_in_dim(seg_ids, first_row, group_rows, 0)
    start_max = jnp.full((groups_here, QPK, group_rows), -1e30, jnp.float32)
    start_total = jnp.zeros((groups_here, QPK, group_rows), jnp.float32)
    start_acc = jnp.zeros((groups_here, QPK, group_rows, HD), jnp.float32)
    carry = (start_max, start_total, start_acc)
    piece = lax.all_gather(keyvals, "seq", axis=0, tiled=True)
    rows = piece.shape[0]
    block = math.gcd(rows, 1024)

    def advance(state, number):
        offset = number * block
        kv_block = lax.dynamic_slice_in_dim(piece, offset, block, 0)
        k_index = offset + jnp.arange(block, dtype=jnp.int32)
        k_seg = lax.dynamic_slice_in_dim(seg_ids, offset, block, 0)
        k_live = lax.dynamic_slice_in_dim(live, offset, block, 0)
        active = (offset <= q_index[-1]) & (k_seg[0] <= q_seg[-1]) & (k_seg[-1] >= q_seg[0])

        def compute(inner):
            run_max, run_total, run_acc = inner
            allowed = (k_seg[None, :] == q_seg[:, None]) & (k_index[None, :] <= q_index[:, None])
            allowed = allowed & ((k_live[None, :] == 1) | (k_index[None, :] == q_index[:, None]))
            scores = (
                jnp.einsum(
                    "qgcd,kgd->gcqk",
                    queries,
                    kv_block[:, :, :HD],
                    preferred_element_type=jnp.float32,
                )
                * 0.015625
            )
            masked = jnp.where(allowed[None, None], scores, -1e30)
            new_max = jnp.maximum(run_max, jnp.max(masked, axis=-1))
            weights = jnp.where(allowed[None, None], jnp.exp(masked - new_max[..., None]), 0.0)
            factor = jnp.exp(run_max - new_max)
            new_total = run_total * factor + jnp.sum(weights, axis=-1)
            update = jnp.einsum(
                "gcqk,kgd->gcqd",
                weights.astype(jnp.bfloat16),
                kv_block[:, :, HD:],
                preferred_element_type=jnp.float32,
            )
            return (new_max, new_total, run_acc * factor[..., None] + update)

        return (lax.cond(active, compute, lambda inner: inner, state), None)

    carry, _ = lax.scan(advance, carry, jnp.arange(rows // block, dtype=jnp.int32))
    final_max, final_total, final_acc = carry
    attended = (final_acc / final_total[..., None]).transpose(2, 0, 1, 3)
    attended = attended.reshape(group_rows, groups_here * QPK * HD).astype(jnp.bfloat16)
    own_tokens = lax.all_to_all(attended, "head", split_axis=0, concat_axis=1, tiled=True)
    mixed = jnp.dot(own_tokens, w_out, preferred_element_type=jnp.float32).astype(jnp.bfloat16)
    page_count = group_rows // PAGE
    pages = keyvals.reshape(page_count, PAGE, groups_here, 2 * HD)
    table_mine = lax.dynamic_slice_in_dim(page_table, seq_at * page_count, page_count, 0)
    order = jnp.argsort(table_mine // page_count, stable=True)
    received = lax.all_to_all(pages[order], "seq", split_axis=0, concat_axis=0, tiled=True)
    arriving = jnp.argsort((page_table // page_count != seq_at).astype(jnp.int32), stable=True)[
        :page_count
    ]
    slots = page_table[arriving] % page_count
    kv_pool = jnp.zeros_like(received).at[slots].set(received).transpose(2, 0, 1, 3)
    return (mixed, kv_pool)


def solution(mesh):
    placed = (P(("seq", "head"), None), P(), P(), P(), P(), P())
    return jax.shard_map(
        shards,
        mesh=mesh,
        in_specs=placed,
        out_specs=(P(("seq", "head"), None), P("head", "seq", None, None)),
        check_vma=False,
    )
```

profile of v0, /device:TPU:71, one launch (start us, length us, event | category | flops | bytes accessed | tf_op | source)
XLA Modules:
  0.0 432.3 jit_solution(488197690336728384)
XLA Ops:
  7.9 92.7 %all-gather.3.cloned.1.call-done = bf16[1024,2048]{1,0:T(8,128)(2,1)} async-done(((bf16[128,2048]{1,0:T(8,128)(2,1)}), bf16[1024,2048]{1,0:T(8,128)(2,1)}) %all-gather.3.cloned.1.call-update) | async-done | bytes 4194320 | tf_op jit(solution)/shard_map/all_gather | solution.py:23
  100.6 4.5 %fusion.23 = bf16[384,1024]{1,0:T(8,128)(2,1)S(1)} fusion(bf16[1024,2048]{1,0:T(8,128)(2,1)} %all-gather.3.cloned.1.call-done, bf16[2048,3072]{1,0:T(8,128)(2,1)} %param.11, s32[]{:T(128)S(6)} %select_n.66), kind=kOutput, calls=%fused_computation.32 | convolution fusion | flops 1611005952 | bytes 6553604 | tf_op jit(solution)/shard_map/dot_general | solution.py:22
  110.1 4.4 %sort.34 = (s32[1024]{0:T(1024)}, s32[1024]{0:T(1024)S(1)}) sort(s32[1024]{0:T(1024)S(1)} %fusion.29, s32[1024]{0:T(1024)S(1)} %iota.19), dimensions={0}, to_apply=%region_6.7 | sort | flops 10240 | bytes 16384 | tf_op jit(solution)/shard_map/jit(argsort)/sort | solution.py:89
  117.4 7.7 %all-to-all-start.1 = ((bf16[64,16,1,128]{3,1,2,0:T(8,128)(2,1)}), bf16[64,16,1,128]{3,1,2,0:T(8,128)(2,1)S(1)}, u32[]{:S(2)}, u32[]{:S(2)}) async-start(bf16[64,16,1,128]{3,1,2,0:T(8,128)(2,1)} %bitcast.28), calls=%async_computation.1 | async-start | bytes 524288 | tf_op jit(solution)/shard_map/all_to_all | solution.py:88
  125.1 38.8 %all-gather.5.cloned.1.call-done = bf16[16384,1,128]{0,2,1:T(8,128)(2,1)} async-done(((bf16[1024,1,128]{0,2,1:T(8,128)(2,1)}), bf16[16384,1,128]{0,2,1:T(8,128)(2,1)}) %all-gather.5.cloned.1.call-update) | async-done | bytes 4194320 | tf_op jit(solution)/shard_map/all_gather | solution.py:38
  164.0 242.2 %while.14 = (s32[]{:T(128)}, f32[1,4,1024]{2,1,0:T(4,128)S(1)}, f32[1,4,1024]{2,1,0:T(4,128)S(1)}, f32[1,4,1024,64]{2,3,1,0:T(8,128)S(1)}, s32[16]{0:T(128)S(1)}...) while((s32[]{:T(128)}, f32[1,4,1024]{2,1,0:T(4,128)S(1)}, ...), condition=%wide.region_5.6_spmd, body=%wide.region_0.5_spmd.sunk | while | flops 1135097856 | bytes 57716176 | solution.py:78
  222.4 17.3 %conditional.2 = ((f32[1,4,1024]{2,1,0:T(4,128)S(1)}, f32[1,4,1024]{2,1,0:T(4,128)S(1)}, f32[1,4,1024,64]{2,3,1,0:T(8,128)S(1)})) conditional(s32[]{:T(128)} %convert_element_type.50, (f32[1,4,1024]{2,1,0:T(4,128)S(1)}, f32[1,4,1024]{2,1,0:T(4,128)S(1)}, f32[1,4,1024,64]{2,3,1,0:T(8,128)S(1)}) %tuple.43, (s32[1024]{0:T(1024)S(1)}, ...), branch_computations={%region_1.1_spmd, %region_2.4_spmd} | conditional | flops 1135097856 | bytes 57703480 | solution.py:76
  224.9 4.3 fusion
  229.2 6.3 %fusion.10 = f32[1,4,1024,64]{2,3,1,0:T(8,128)S(1)} fusion(f32[1024,1024,4]{1,0,2:T(8,128)S(1)} %get-tuple-element.193, f32[4,1024]{1,0:T(4,128)S(1)} %bitcast.95, pred[1024,1024]{0,1:T(8,128)(4,1)S(1)} %or_and_fusion, f32[1,4,1024,64]{2,3,1,0:T(8,128)S(1)} %get-tuple-element.142, f32[4,1024]{1,0:T(4,128)S(1)} %get-tuple-element.190, ...), kind=kOutput, calls=%fused_computation.13 | convolution fusion | flops 558366720 | bytes 20087300 | tf_op jit(solution)/shard_map/while/body/eval_jaxpr/cond/branch_1_fun/gcqk,kgd->gcqd/dot_general | solution.py:68
  246.2 17.3 %conditional.2 = ((f32[1,4,1024]{2,1,0:T(4,128)S(1)}, f32[1,4,1024]{2,1,0:T(4,128)S(1)}, f32[1,4,1024,64]{2,3,1,0:T(8,128)S(1)})) conditional(s32[]{:T(128)} %convert_element_type.50, (f32[1,4,1024]{2,1,0:T(4,128)S(1)}, f32[1,4,1024]{2,1,0:T(4,128)S(1)}, f32[1,4,1024,64]{2,3,1,0:T(8,128)S(1)}) %tuple.43, (s32[1024]{0:T(1024)S(1)}, ...), branch_computations={%region_1.1_spmd, %region_2.4_spmd} | conditional | flops 1135097856 | bytes 57703480 | solution.py:76
  248.7 4.3 fusion
  253.0 6.3 %fusion.10 = f32[1,4,1024,64]{2,3,1,0:T(8,128)S(1)} fusion(f32[1024,1024,4]{1,0,2:T(8,128)S(1)} %get-tuple-element.193, f32[4,1024]{1,0:T(4,128)S(1)} %bitcast.95, pred[1024,1024]{0,1:T(8,128)(4,1)S(1)} %or_and_fusion, f32[1,4,1024,64]{2,3,1,0:T(8,128)S(1)} %get-tuple-element.142, f32[4,1024]{1,0:T(4,128)S(1)} %get-tuple-element.190, ...), kind=kOutput, calls=%fused_computation.13 | convolution fusion | flops 558366720 | bytes 20087300 | tf_op jit(solution)/shard_map/while/body/eval_jaxpr/cond/branch_1_fun/gcqk,kgd->gcqd/dot_general | solution.py:68
  270.0 17.3 %conditional.2 = ((f32[1,4,1024]{2,1,0:T(4,128)S(1)}, f32[1,4,1024]{2,1,0:T(4,128)S(1)}, f32[1,4,1024,64]{2,3,1,0:T(8,128)S(1)})) conditional(s32[]{:T(128)} %convert_element_type.50, (f32[1,4,1024]{2,1,0:T(4,128)S(1)}, f32[1,4,1024]{2,1,0:T(4,128)S(1)}, f32[1,4,1024,64]{2,3,1,0:T(8,128)S(1)}) %tuple.43, (s32[1024]{0:T(1024)S(1)}, ...), branch_computations={%region_1.1_spmd, %region_2.4_spmd} | conditional | flops 1135097856 | bytes 57703480 | solution.py:76
  272.5 4.3 fusion
  276.8 6.3 %fusion.10 = f32[1,4,1024,64]{2,3,1,0:T(8,128)S(1)} fusion(f32[1024,1024,4]{1,0,2:T(8,128)S(1)} %get-tuple-element.193, f32[4,1024]{1,0:T(4,128)S(1)} %bitcast.95, pred[1024,1024]{0,1:T(8,128)(4,1)S(1)} %or_and_fusion, f32[1,4,1024,64]{2,3,1,0:T(8,128)S(1)} %get-tuple-element.142, f32[4,1024]{1,0:T(4,128)S(1)} %get-tuple-element.190, ...), kind=kOutput, calls=%fused_computation.13 | convolution fusion | flops 558366720 | bytes 20087300 | tf_op jit(solution)/shard_map/while/body/eval_jaxpr/cond/branch_1_fun/gcqk,kgd->gcqd/dot_general | solution.py:68
  293.7 17.3 %conditional.2 = ((f32[1,4,1024]{2,1,0:T(4,128)S(1)}, f32[1,4,1024]{2,1,0:T(4,128)S(1)}, f32[1,4,1024,64]{2,3,1,0:T(8,128)S(1)})) conditional(s32[]{:T(128)} %convert_element_type.50, (f32[1,4,1024]{2,1,0:T(4,128)S(1)}, f32[1,4,1024]{2,1,0:T(4,128)S(1)}, f32[1,4,1024,64]{2,3,1,0:T(8,128)S(1)}) %tuple.43, (s32[1024]{0:T(1024)S(1)}, ...), branch_computations={%region_1.1_spmd, %region_2.4_spmd} | conditional | flops 1135097856 | bytes 57703480 | solution.py:76
  296.3 4.3 fusion
  300.6 6.3 %fusion.10 = f32[1,4,1024,64]{2,3,1,0:T(8,128)S(1)} fusion(f32[1024,1024,4]{1,0,2:T(8,128)S(1)} %get-tuple-element.193, f32[4,1024]{1,0:T(4,128)S(1)} %bitcast.95, pred[1024,1024]{0,1:T(8,128)(4,1)S(1)} %or_and_fusion, f32[1,4,1024,64]{2,3,1,0:T(8,128)S(1)} %get-tuple-element.142, f32[4,1024]{1,0:T(4,128)S(1)} %get-tuple-element.190, ...), kind=kOutput, calls=%fused_computation.13 | convolution fusion | flops 558366720 | bytes 20087300 | tf_op jit(solution)/shard_map/while/body/eval_jaxpr/cond/branch_1_fun/gcqk,kgd->gcqd/dot_general | solution.py:68
  317.5 17.3 %conditional.2 = ((f32[1,4,1024]{2,1,0:T(4,128)S(1)}, f32[1,4,1024]{2,1,0:T(4,128)S(1)}, f32[1,4,1024,64]{2,3,1,0:T(8,128)S(1)})) conditional(s32[]{:T(128)} %convert_element_type.50, (f32[1,4,1024]{2,1,0:T(4,128)S(1)}, f32[1,4,1024]{2,1,0:T(4,128)S(1)}, f32[1,4,1024,64]{2,3,1,0:T(8,128)S(1)}) %tuple.43, (s32[1024]{0:T(1024)S(1)}, ...), branch_computations={%region_1.1_spmd, %region_2.4_spmd} | conditional | flops 1135097856 | bytes 57703480 | solution.py:76
  320.0 4.3 fusion
  324.4 6.3 %fusion.10 = f32[1,4,1024,64]{2,3,1,0:T(8,128)S(1)} fusion(f32[1024,1024,4]{1,0,2:T(8,128)S(1)} %get-tuple-element.193, f32[4,1024]{1,0:T(4,128)S(1)} %bitcast.95, pred[1024,1024]{0,1:T(8,128)(4,1)S(1)} %or_and_fusion, f32[1,4,1024,64]{2,3,1,0:T(8,128)S(1)} %get-tuple-element.142, f32[4,1024]{1,0:T(4,128)S(1)} %get-tuple-element.190, ...), kind=kOutput, calls=%fused_computation.13 | convolution fusion | flops 558366720 | bytes 20087300 | tf_op jit(solution)/shard_map/while/body/eval_jaxpr/cond/branch_1_fun/gcqk,kgd->gcqd/dot_general | solution.py:68
  341.3 17.3 %conditional.2 = ((f32[1,4,1024]{2,1,0:T(4,128)S(1)}, f32[1,4,1024]{2,1,0:T(4,128)S(1)}, f32[1,4,1024,64]{2,3,1,0:T(8,128)S(1)})) conditional(s32[]{:T(128)} %convert_element_type.50, (f32[1,4,1024]{2,1,0:T(4,128)S(1)}, f32[1,4,1024]{2,1,0:T(4,128)S(1)}, f32[1,4,1024,64]{2,3,1,0:T(8,128)S(1)}) %tuple.43, (s32[1024]{0:T(1024)S(1)}, ...), branch_computations={%region_1.1_spmd, %region_2.4_spmd} | conditional | flops 1135097856 | bytes 57703480 | solution.py:76
  343.8 4.3 fusion
  348.1 6.3 %fusion.10 = f32[1,4,1024,64]{2,3,1,0:T(8,128)S(1)} fusion(f32[1024,1024,4]{1,0,2:T(8,128)S(1)} %get-tuple-element.193, f32[4,1024]{1,0:T(4,128)S(1)} %bitcast.95, pred[1024,1024]{0,1:T(8,128)(4,1)S(1)} %or_and_fusion, f32[1,4,1024,64]{2,3,1,0:T(8,128)S(1)} %get-tuple-element.142, f32[4,1024]{1,0:T(4,128)S(1)} %get-tuple-element.190, ...), kind=kOutput, calls=%fused_computation.13 | convolution fusion | flops 558366720 | bytes 20087300 | tf_op jit(solution)/shard_map/while/body/eval_jaxpr/cond/branch_1_fun/gcqk,kgd->gcqd/dot_general | solution.py:68
  365.1 17.3 %conditional.2 = ((f32[1,4,1024]{2,1,0:T(4,128)S(1)}, f32[1,4,1024]{2,1,0:T(4,128)S(1)}, f32[1,4,1024,64]{2,3,1,0:T(8,128)S(1)})) conditional(s32[]{:T(128)} %convert_element_type.50, (f32[1,4,1024]{2,1,0:T(4,128)S(1)}, f32[1,4,1024]{2,1,0:T(4,128)S(1)}, f32[1,4,1024,64]{2,3,1,0:T(8,128)S(1)}) %tuple.43, (s32[1024]{0:T(1024)S(1)}, ...), branch_computations={%region_1.1_spmd, %region_2.4_spmd} | conditional | flops 1135097856 | bytes 57703480 | solution.py:76
  367.6 4.3 fusion
  371.9 6.3 %fusion.10 = f32[1,4,1024,64]{2,3,1,0:T(8,128)S(1)} fusion(f32[1024,1024,4]{1,0,2:T(8,128)S(1)} %get-tuple-element.193, f32[4,1024]{1,0:T(4,128)S(1)} %bitcast.95, pred[1024,1024]{0,1:T(8,128)(4,1)S(1)} %or_and_fusion, f32[1,4,1024,64]{2,3,1,0:T(8,128)S(1)} %get-tuple-element.142, f32[4,1024]{1,0:T(4,128)S(1)} %get-tuple-element.190, ...), kind=kOutput, calls=%fused_computation.13 | convolution fusion | flops 558366720 | bytes 20087300 | tf_op jit(solution)/shard_map/while/body/eval_jaxpr/cond/branch_1_fun/gcqk,kgd->gcqd/dot_general | solution.py:68
  388.9 17.3 %conditional.2 = ((f32[1,4,1024]{2,1,0:T(4,128)S(1)}, f32[1,4,1024]{2,1,0:T(4,128)S(1)}, f32[1,4,1024,64]{2,3,1,0:T(8,128)S(1)})) conditional(s32[]{:T(128)} %convert_element_type.50, (f32[1,4,1024]{2,1,0:T(4,128)S(1)}, f32[1,4,1024]{2,1,0:T(4,128)S(1)}, f32[1,4,1024,64]{2,3,1,0:T(8,128)S(1)}) %tuple.43, (s32[1024]{0:T(1024)S(1)}, ...), branch_computations={%region_1.1_spmd, %region_2.4_spmd} | conditional | flops 1135097856 | bytes 57703480 | solution.py:76
  391.4 4.3 fusion
  395.7 6.3 %fusion.10 = f32[1,4,1024,64]{2,3,1,0:T(8,128)S(1)} fusion(f32[1024,1024,4]{1,0,2:T(8,128)S(1)} %get-tuple-element.193, f32[4,1024]{1,0:T(4,128)S(1)} %bitcast.95, pred[1024,1024]{0,1:T(8,128)(4,1)S(1)} %or_and_fusion, f32[1,4,1024,64]{2,3,1,0:T(8,128)S(1)} %get-tuple-element.142, f32[4,1024]{1,0:T(4,128)S(1)} %get-tuple-element.190, ...), kind=kOutput, calls=%fused_computation.13 | convolution fusion | flops 558366720 | bytes 20087300 | tf_op jit(solution)/shard_map/while/body/eval_jaxpr/cond/branch_1_fun/gcqk,kgd->gcqd/dot_general | solution.py:68
  407.3 5.6 %all-to-all-start = ((bf16[8,128,256]{1,2,0:T(8,128)(2,1)}), bf16[8,128,256]{1,2,0:T(8,128)(2,1)S(1)}, u32[]{:S(2)}, u32[]{:S(2)}) async-start(bf16[8,128,256]{1,2,0:T(8,128)(2,1)} %copy.15), calls=%async_computation | async-start | bytes 1048576 | tf_op jit(solution)/shard_map/all_to_all | solution.py:82
  420.0 5.5 %convolution_convert_fusion = bf16[128,2048]{1,0:T(8,128)(2,1)} fusion(bf16[128,2048]{0,1:T(8,128)(2,1)S(1)} %bitcast.97, bf16[2048,2048]{1,0:T(8,128)(2,1)} %param.12), kind=kOutput, calls=%fused_computation.29 | convolution fusion | flops 1074003968 | bytes 9437184 | tf_op jit(solution)/shard_map/dot_general | solution.py:83
  (181 shorter events, 111.0 us)
Async XLA Ops:
  7.2 93.5 %all-gather.3.cloned.1.call-start = ((), (), s32[]{:S(2)}) async-start(), calls=%async_computation.2 | async-start | bytes 4718592 | tf_op jit(solution)/shard_map/all_gather | solution.py:23
  7.9 156.0 %all-gather.5.cloned.1.call-start = ((), (), s32[]{:S(2)}) async-start(), calls=%async_computation.3 | async-start | bytes 4456448 | tf_op jit(solution)/shard_map/all_gather | solution.py:38
  117.4 289.9 %all-to-all-start.1 = ((bf16[64,16,1,128]{3,1,2,0:T(8,128)(2,1)}), bf16[64,16,1,128]{3,1,2,0:T(8,128)(2,1)S(1)}, u32[]{:S(2)}, u32[]{:S(2)}) async-start(bf16[64,16,1,128]{3,1,2,0:T(8,128)(2,1)} %bitcast.28), calls=%async_computation.1 | async-start | bytes 524288 | tf_op jit(solution)/shard_map/all_to_all | solution.py:88
  164.0 248.9 %copy-start = (s32[1024]{0:T(1024)S(1)}, s32[1024]{0:T(1024)}, u32[]{:S(2)}) copy-start(s32[1024]{0:T(1024)} %param.15) | copy-start | bytes 12292
  407.3 12.6 %all-to-all-start = ((bf16[8,128,256]{1,2,0:T(8,128)(2,1)}), bf16[8,128,256]{1,2,0:T(8,128)(2,1)S(1)}, u32[]{:S(2)}, u32[]{:S(2)}) async-start(bf16[8,128,256]{1,2,0:T(8,128)(2,1)} %copy.15), calls=%async_computation | async-start | bytes 1048576 | tf_op jit(solution)/shard_map/all_to_all | solution.py:82
  416.2 9.2 %copy-start.1 = (bf16[64,16,128]{2,1,0:T(8,128)(2,1)}, bf16[64,16,128]{2,1,0:T(8,128)(2,1)S(1)}, u32[]{:S(2)}) copy-start(bf16[64,16,128]{2,1,0:T(8,128)(2,1)S(1)} %scatter_fusion) | copy-start | bytes 786436
Sparse Core Ops, SparseCore 0:
  9.6 90.9 all-gather.2
  106.0 57.8 all-gather.4
where the time goes:
time: 435 us; the launch traced here: 432 us
  waiting for transfers between devices  136 us (31%)
  matrix products  94.3 us (22%)
  loops' own time  63.7 us (15%)
  other arithmetic  61.7 us (14%)
  local copies, waits for them, and re-layouts  49.1 us (11%)
  between operations  14.2 us (3%)
  starting transfers between devices  13.4 us (3%)
    all_gather x1, waiting for transfers between devices, shards(): lax.all_gather(hidden, 'head', axis=0, tiled=True)  92.7 us
    another operation x1, loops' own time, shards(): lax.scan(advance, carry, jnp.arange(rows // block, dtype=jnp.int32))  63.1 us
    dot_general x8, matrix products, compute(): jnp.einsum('gcqk,kgd->gcqd', weights.astype(jnp.bfloat16), kv_block[:, :,...  50.1 us
    all_gather x1, waiting for transfers between devices, shards(): piece = lax.all_gather(keyvals, 'seq', axis=0, tiled=True)  38.8 us
    dot_general x8, matrix products, compute(): jnp.einsum('qgcd,kgd->gcqk', queries, kv_block[:, :, :HD], preferred_elem...  34.2 us
    reduce_sum x8, other arithmetic, compute(): new_total = run_total * factor + jnp.sum(weights, axis=-1)  33.5 us
    and x8, other arithmetic, compute(): allowed & ((k_live[None, :] == 1) | (k_index[None, :] == q_index[:, None]))  13.6 us
    dynamic_slice x16, local copies, waits for them, and re-layouts, advance(): k_seg = lax.dynamic_slice_in_dim(seg_ids, offset, block, 0)  11.1 us
  transfers between devices with their start and end apart: 4, of which 3 were waited for; matrix products, arithmetic and copies ran while one was open for 45% of the time, Pallas kernels for 0%

commit v1 on v0

v1 whole, which is shorter than its diff:
```python
import functools

import jax
import jax.numpy as jnp
from jax import lax
from jax.experimental import pallas as pl
from jax.experimental.pallas import tpu as pltpu
from jax.sharding import PartitionSpec as P

D = 2048
TOKENS = 16384
KVH = 8
HD = 64
QPK = 4
PAGE = 16
SEQ = 16
ROWS = 128
GT = 1024
COLS = (QPK + 2) * HD
STRIPES = 8
BK = 512
PAD = BK
NEG = -1e30
MESH = pl.DeviceIdType.MESH
bf16, f32 = jnp.bfloat16, jnp.float32


def dealt(s, j):
    slot = (s % 2) * 8 + j
    return jnp.where((s // 2) % 2 == 0, slot, 15 - slot)


def held(s, k):
    slot = s if k % 2 == 0 else 15 - s
    return 2 * k + slot // 8, slot % 8


def project(hid, w, q_out, kv_out, hv, wk, wq, kvs, qs, load, a2a_s, a2a_r, q_s, q_r, g_s, g_r, loc):
    s, j = lax.axis_index("seq"), lax.axis_index("head")
    zh, x, c = s // 8, (s // 2) % 4, s % 2
    to = dealt(s, j)
    mine = to == s

    first = pltpu.make_async_copy(hid, hv, load.at[16])
    first.start()
    loads = []
    for r in range(8):
        g = lax.rem(j + r + 1, 8)
        col = pl.multiple_of(g * COLS + QPK * HD, 128)
        loads.append(pltpu.make_async_copy(w.at[:, pl.ds(col, 2 * HD)], wk.at[r], load.at[r]))
        loads[-1].start()
    for r in range(8):
        g = lax.rem(j + r + 1, 8)
        col = pl.multiple_of(g * COLS, 128)
        loads.append(pltpu.make_async_copy(w.at[:, pl.ds(col, QPK * HD)], wq.at[r], load.at[8 + r]))
        loads[-1].start()

    def block(zz, xx, cc):
        return zz * 8 + xx * 2 + cc

    right, left = lax.rem(x + 1, 4), lax.rem(x + 3, 4)
    far = lax.rem(x + 2, 4)
    peers = [(block(zh, right, c), j), (block(zh, left, c), j), (block(1 - zh, x, c), j), (block(zh, x, 1 - c), j)]

    barrier = pltpu.get_barrier_semaphore()
    for p in peers:
        pl.semaphore_signal(barrier, inc=1, device_id=p, device_id_type=MESH)
    for r in range(7):
        pl.semaphore_signal(barrier, inc=1, device_id=(s, lax.rem(j + r + 1, 8)), device_id_type=MESH)
    for k in range(STRIPES):
        own = mine & (s // 2 == k)

        @pl.when(jnp.logical_not(own))
        def _():
            pl.semaphore_signal(barrier, inc=1, device_id=held(s, k), device_id_type=MESH)

    first.wait()

    row0 = pl.multiple_of(s * GT + j * ROWS, ROWS)
    sends = []
    for r in range(8):
        g = lax.rem(j + r + 1, 8)
        loads[r].wait()
        kvs[r] = jnp.dot(hv[...], wk[r], preferred_element_type=f32).astype(bf16)
        if r == 0:
            pl.semaphore_wait(barrier, jnp.where(mine, 18, 19))

        if r < 7:
            cp = pltpu.make_async_remote_copy(
                src_ref=kvs.at[r],
                dst_ref=kv_out.at[pl.ds(row0, ROWS)],
                send_sem=a2a_s.at[r],
                recv_sem=a2a_r.at[r],
                device_id=(s, g),
                device_id_type=MESH,
            )
            cp.start()
            sends.append(cp)
        else:
            own_kv = pltpu.make_async_copy(kvs.at[r], kv_out.at[pl.ds(row0, ROWS)], loc)
            own_kv.start()

    slot = s // 2
    qsends = []
    for r in range(8):
        g = lax.rem(j + r + 1, 8)
        loads[8 + r].wait()
        qs[r] = (jnp.dot(hv[...], wq[r], preferred_element_type=f32).astype(bf16) * 0.015625).astype(bf16)
        cp = pltpu.make_async_remote_copy(
            src_ref=qs.at[r],
            dst_ref=q_out.at[slot],
            send_sem=q_s.at[r],
            recv_sem=q_r.at[slot],
            device_id=(to, g),
            device_id_type=MESH,
        )
        qsends.append(cp)
        if r < 7:
            cp.start()
        else:

            @pl.when(jnp.logical_not(mine))
            def _():
                cp.start()

            @pl.when(mine)
            def _():
                pltpu.make_async_copy(qs.at[7], q_out.at[slot], q_r.at[slot]).start()

    def rows(b, first_row, count):
        return kv_out.at[pl.ds(pl.multiple_of(b * GT + first_row, 128), count)]

    def arrived(b, first_row, count, i):
        there = rows(b, first_row, count)
        pltpu.make_async_copy(there, there, g_r.at[i]).wait()

    def pass_on(b, first_row, count, i, peer):
        there = rows(b, first_row, count)
        cp = pltpu.make_async_remote_copy(
            src_ref=there,
            dst_ref=there,
            send_sem=g_s.at[i],
            recv_sem=g_r.at[i],
            device_id=peers[peer],
            device_id_type=MESH,
        )
        cp.start()
        sends.append(cp)

    R, L, Z, C = range(4)
    own_kv.wait()
    for r in range(7):
        source = lax.rem(j + 7 - r, 8)
        there = kv_out.at[pl.ds(pl.multiple_of(s * GT + source * ROWS, ROWS), ROWS)]
        pltpu.make_async_copy(there, there, a2a_r.at[r]).wait()
    H = GT // 2
    me = block(zh, x, c)
    pass_on(me, 0, GT, 0, R)
    pass_on(me, 0, GT, 1, L)
    pass_on(me, 0, GT, 2, Z)
    pass_on(me, 0, GT, 3, C)
    bl, br, bf = block(zh, left, c), block(zh, right, c), block(zh, far, c)
    zm, zl, zr, zf = block(1 - zh, x, c), block(1 - zh, left, c), block(1 - zh, right, c), block(1 - zh, far, c)
    arrived(bl, 0, GT, 0)
    pass_on(bl, 0, H, 4, R)
    pass_on(bl, 0, GT, 6, C)
    arrived(br, 0, GT, 1)
    pass_on(br, H, H, 5, L)
    pass_on(br, 0, GT, 7, C)
    arrived(zm, 0, GT, 2)
    pass_on(zm, 0, GT, 10, R)
    pass_on(zm, 0, GT, 11, L)
    pass_on(zm, 0, GT, 12, C)
    arrived(bf, 0, H, 4)
    pass_on(bf, 0, H, 8, C)
    arrived(bf, H, H, 5)
    pass_on(bf, H, H, 9, C)
    arrived(zl, 0, GT, 10)
    pass_on(zl, 0, H, 13, R)
    pass_on(zl, 0, GT, 15, C)
    arrived(zr, 0, GT, 11)
    pass_on(zr, H, H, 14, L)
    pass_on(zr, 0, GT, 16, C)
    arrived(zf, 0, H, 13)
    pass_on(zf, 0, H, 17, C)
    arrived(zf, H, H, 14)
    pass_on(zf, H, H, 18, C)
    d = 1 - c
    arrived(block(zh, x, d), 0, GT, 3)
    arrived(block(zh, left, d), 0, GT, 6)
    arrived(block(zh, right, d), 0, GT, 7)
    arrived(block(zh, far, d), 0, H, 8)
    arrived(block(zh, far, d), H, H, 9)
    arrived(block(1 - zh, x, d), 0, GT, 12)
    arrived(block(1 - zh, left, d), 0, GT, 15)
    arrived(block(1 - zh, right, d), 0, GT, 16)
    arrived(block(1 - zh, far, d), 0, H, 17)
    arrived(block(1 - zh, far, d), H, H, 18)

    for k in range(STRIPES):
        pltpu.make_async_copy(q_out.at[k], q_out.at[k], q_r.at[k]).wait()
    for cp in sends + qsends[:7]:
        cp.wait_send()

    @pl.when(jnp.logical_not(mine))
    def _():
        qsends[7].wait_send()


def attend(count, seg0, inv, code, q, kv_hbm, att, pool, kv, ve, qe, m, acc, sem, page_sem):
    s = lax.axis_index("seq")
    chunk = TOKENS // STRIPES

    def load(k):
        at = pl.multiple_of(k * chunk, chunk)
        return pltpu.make_async_copy(
            kv_hbm.at[pl.ds(at, chunk)], kv.at[pl.ds(pl.multiple_of(PAD + at, 128), chunk)], sem.at[k]
        )

    for k in range(STRIPES):
        load(k).start()

    @pl.loop(0, TOKENS // PAGE // SEQ)
    def _(i):
        at = pl.multiple_of(inv[i] * PAGE, PAGE)
        pltpu.make_async_copy(kv_hbm.at[pl.ds(at, PAGE)], pool.at[pl.ds(pl.multiple_of(i * PAGE, PAGE), PAGE)], page_sem).start()

    kv[:PAD] = jnp.zeros((PAD, 2 * HD), bf16)
    ve[:PAD] = jnp.zeros((PAD, 2 * HD), bf16)
    low = lax.broadcasted_iota(jnp.int32, (1, 2 * HD), 1) < HD
    it = lax.broadcasted_iota(jnp.int32, (ROWS, ROWS), 0)
    iu = lax.broadcasted_iota(jnp.int32, (ROWS, ROWS), 1)

    def scores(c, keys):
        return lax.dot_general(qe[c], keys, (((1,), (1,)), ((), ())), preferred_element_type=f32)

    @pl.loop(0, STRIPES)
    def _(k):
        load(k).wait()

        @pl.loop(0, chunk // 256)
        def _(i):
            at = pl.ds(pl.multiple_of(PAD + k * chunk + i * 256, 256), 256)
            ve[at] = jnp.where(low, jnp.ones((256, 2 * HD), bf16), kv[at])

        slot = jnp.where(k % 2 == 0, s, 15 - s)
        stripe = 16 * k + slot
        t0 = stripe * ROWS
        own = seg0[k]
        zero = jnp.zeros((ROWS, HD), bf16)
        for c in range(QPK):
            qe[c] = jnp.concatenate([q[k, :, c * HD : (c + 1) * HD], zero], axis=1)

        here = pl.ds(pl.multiple_of(PAD + t0, 128), ROWS)
        cu = jnp.broadcast_to(code[pl.ds(PAD // 128 + stripe, 1), :], (ROWS, ROWS))
        ct = cu.T
        allowed = ((cu & 15) == (ct & 15)) & (iu <= it) & ((cu < 16) | (iu == it))
        same = (ct[:, :1] & 15) == own
        for c in range(QPK):
            sc = jnp.where(allowed, scores(c, kv[here]), NEG)
            top = jnp.max(sc, axis=1, keepdims=True)
            p = jnp.exp(sc - top)
            acc[c] = jnp.dot(p.astype(bf16), ve[here], preferred_element_type=f32)
            m[c] = jnp.where(same, top, -NEG)

        @pl.loop(0, count[k])
        def _(i):
            first = PAD + t0 - (i + 1) * BK
            at = pl.ds(pl.multiple_of(first, 128), BK)
            bias = [
                jnp.where(code[pl.ds(first // 128 + n, 1), :] == own, 0.0, NEG) for n in range(BK // 128)
            ]
            bias = jnp.concatenate(bias, axis=1)
            for c in range(QPK):
                sc = scores(c, kv[at]) + bias
                old = m[c]
                top = jnp.maximum(old, jnp.max(sc, axis=1, keepdims=True))
                p = jnp.exp(sc - top)
                acc[c] = acc[c] * jnp.exp(old - top) + jnp.dot(p.astype(bf16), ve[at], preferred_element_type=f32)
                m[c] = top

        for c in range(0, QPK, 2):
            a, b = acc[c], acc[c + 1]
            first_head = pltpu.roll(a, HD, 1) / a
            second_head = b / pltpu.roll(b, HD, 1)
            att[k, :, c * HD : (c + 2) * HD] = jnp.where(low, first_head, second_head).astype(bf16)

    pltpu.make_async_copy(kv_hbm.at[pl.ds(0, GT)], pool, page_sem).wait()


def mix(att, w, out, wv, got, acc, load, a_s, a_r):
    s, j = lax.axis_index("seq"), lax.axis_index("head")
    to = dealt(s, j)
    mine = to == s
    loads = []
    for r in range(8):
        h = lax.rem(j + 8 - r, 8)
        at = pl.multiple_of(h * QPK * HD, QPK * HD)
        loads.append(pltpu.make_async_copy(w.at[pl.ds(at, QPK * HD)], wv.at[r], load.at[r]))
        loads[-1].start()

    barrier = pltpu.get_barrier_semaphore()
    for r in range(8):
        h = lax.rem(j + r + 1, 8)
        if r < 7:
            pl.semaphore_signal(barrier, inc=1, device_id=(to, h), device_id_type=MESH)
        else:

            @pl.when(jnp.logical_not(mine))
            def _():
                pl.semaphore_signal(barrier, inc=1, device_id=(to, h), device_id_type=MESH)

    pl.semaphore_wait(barrier, jnp.where(mine, 7, 8))

    copies = []
    for k in range(STRIPES):
        own = mine & (s // 2 == k)
        cp = pltpu.make_async_remote_copy(
            src_ref=att.at[k],
            dst_ref=got.at[j],
            send_sem=a_s.at[k],
            recv_sem=a_r.at[j],
            device_id=held(s, k),
            device_id_type=MESH,
        )
        copies.append((own, cp))

        @pl.when(jnp.logical_not(own))
        def _():
            cp.start()

        @pl.when(own)
        def _():
            pltpu.make_async_copy(att.at[k], got.at[j], a_r.at[j]).start()

    for r in range(8):
        h = lax.rem(j + 8 - r, 8)
        loads[r].wait()
        pltpu.make_async_copy(got.at[h], got.at[h], a_r.at[h]).wait()
        part = jnp.dot(got[h], wv[r], preferred_element_type=f32)
        if r == 0:
            acc[...] = part
        elif r < 7:
            acc[...] += part
        else:
            out[...] = (acc[...] + part).astype(bf16)
    for own, cp in copies:

        @pl.when(jnp.logical_not(own))
        def _():
            cp.wait_send()


ANY = pl.BlockSpec(memory_space=pl.ANY)
SMEM = pl.BlockSpec(memory_space=pltpu.SMEM)
VMEM = pl.BlockSpec(memory_space=pltpu.VMEM)
DMA = pltpu.SemaphoreType.DMA


def shards(hidden, w_qkv, w_out, seg_ids, live, page_table):
    s = lax.axis_index("seq")
    q, kv = pl.pallas_call(
        project,
        out_shape=(
            jax.ShapeDtypeStruct((STRIPES, ROWS, QPK * HD), bf16),
            jax.ShapeDtypeStruct((TOKENS, 2 * HD), bf16),
        ),
        in_specs=[ANY, ANY],
        out_specs=(ANY, ANY),
        scratch_shapes=[
            pltpu.VMEM((ROWS, D), bf16),
            pltpu.VMEM((KVH, D, 2 * HD), bf16),
            pltpu.VMEM((KVH, D, QPK * HD), bf16),
            pltpu.VMEM((KVH, ROWS, 2 * HD), bf16),
            pltpu.VMEM((KVH, ROWS, QPK * HD), bf16),
            DMA((17,)),
            DMA((7,)),
            DMA((7,)),
            DMA((8,)),
            DMA((8,)),
            DMA((19,)),
            DMA((19,)),
            DMA,
        ],
        compiler_params=pltpu.CompilerParams(collective_id=0, has_side_effects=True, vmem_limit_bytes=40 << 20),
        name="project",
    )(hidden, w_qkv)

    heads = seg_ids.reshape(STRIPES, SEQ, ROWS)[:, :, 0]
    even = lax.dynamic_slice_in_dim(heads, s, 1, 1)[:, 0]
    odd = lax.dynamic_slice_in_dim(heads, 15 - s, 1, 1)[:, 0]
    number = jnp.arange(STRIPES, dtype=jnp.int32)
    is_even = number % 2 == 0
    seg0 = jnp.where(is_even, even, odd)
    begin = jnp.sum((seg_ids[None, :] < seg0[:, None]).astype(jnp.int32), axis=1)
    t0 = (16 * number + jnp.where(is_even, s, 15 - s)) * ROWS
    count = (t0 - begin + BK - 1) // BK
    page = s * (TOKENS // PAGE // SEQ) + jnp.arange(TOKENS // PAGE // SEQ, dtype=jnp.int32)
    inv = jnp.sum(
        jnp.where(page_table[None, :] == page[:, None], jnp.arange(TOKENS // PAGE, dtype=jnp.int32)[None, :], 0), axis=1
    )
    code = (seg_ids + 16 * (1 - live)).reshape(TOKENS // 128, 128)
    code = jnp.concatenate([jnp.full((PAD // 128, 128), 255, jnp.int32), code], axis=0)

    att, pool = pl.pallas_call(
        attend,
        out_shape=(
            jax.ShapeDtypeStruct((STRIPES, ROWS, QPK * HD), bf16),
            jax.ShapeDtypeStruct((GT, 2 * HD), bf16),
        ),
        in_specs=[SMEM, SMEM, SMEM, VMEM, VMEM, ANY],
        out_specs=(VMEM, ANY),
        scratch_shapes=[
            pltpu.VMEM((PAD + TOKENS, 2 * HD), bf16),
            pltpu.VMEM((PAD + TOKENS, 2 * HD), bf16),
            pltpu.VMEM((QPK, ROWS, 2 * HD), bf16),
            pltpu.VMEM((QPK, ROWS, 1), f32),
            pltpu.VMEM((QPK, ROWS, 2 * HD), f32),
            DMA((STRIPES,)),
            DMA,
        ],
        compiler_params=pltpu.CompilerParams(vmem_limit_bytes=40 << 20),
        name="attend",
    )(count, seg0, inv, code, q, kv)

    mixed = pl.pallas_call(
        mix,
        out_shape=jax.ShapeDtypeStruct((ROWS, D), bf16),
        in_specs=[ANY, ANY],
        out_specs=VMEM,
        scratch_shapes=[
            pltpu.VMEM((KVH, QPK * HD, D), bf16),
            pltpu.VMEM((KVH, ROWS, QPK * HD), bf16),
            pltpu.VMEM((ROWS, D), f32),
            DMA((8,)),
            DMA((8,)),
            DMA((8,)),
        ],
        compiler_params=pltpu.CompilerParams(collective_id=1, has_side_effects=True, vmem_limit_bytes=40 << 20),
        name="mix",
    )(att, w_out)
    return mixed, pool.reshape(1, TOKENS // PAGE // SEQ, PAGE, 2 * HD)


def solution(mesh):
    placed = (P(("seq", "head"), None), P(), P(), P(), P(), P())
    return jax.shard_map(
        shards,
        mesh=mesh,
        in_specs=placed,
        out_specs=(P(("seq", "head"), None), P("head", "seq", None, None)),
        check_vma=False,
    )
```

time: 435 us -> 149 us (0.34)
  the two profiles are of different devices: /device:TPU:71 before, /device:TPU:5 now
where the time goes in v1:
time: 149 us
  Pallas kernels  142 us (95%)
  local copies, waits for them, and re-layouts  3.17 us (2%)
  other arithmetic  2.96 us (2%)
    pallas_call x1, Pallas kernels, shards(): pl.pallas_call(attend, out_shape=(jax.ShapeDtypeStruct((STRIPES, ROWS, QP...  75.3 us
    pallas_call x1, Pallas kernels, shards(): pl.pallas_call(project, out_shape=(jax.ShapeDtypeStruct((STRIPES, ROWS, Q...  44.9 us
    pallas_call x1, Pallas kernels, shards(): pl.pallas_call(mix, out_shape=jax.ShapeDtypeStruct((ROWS, D), bf16), in_s...  21.8 us

profile of v1, /device:TPU:5, one launch (start us, length us, event | category | flops | bytes accessed | tf_op | source)
XLA Modules:
  0.0 148.8 jit_solution(3014352564283338558)
XLA Ops:
  0.6 0.9 select_reduce_fusion.inv
  1.5 1.2 dynamic-slice_reduce_fusion
  2.7 1.2 convert_reduce_fusion
  3.9 0.9 add_bitcast_fusion
  4.8 0.0 slice-start
  4.8 0.0 copy-start
  4.8 1.2 copy-done
  6.0 0.0 slice-start.1
  6.0 44.9 %project.1 = (bf16[8,128,256]{2,1,0:T(8,128)(2,1)S(1)}, bf16[16384,128]{1,0:T(8,128)(2,1)S(1)}) custom-call(bf16[128,2048]{1,0:T(8,128)(2,1)S(1)} %copy-done, bf16[2048,3072]{1,0:T(8,128)(2,1)} %w.2), custom_call_target="tpu_custom_call" | custom-call | tf_op jit(solution)/shard_map/project/pallas_call | solution.py:362
  50.9 75.3 %attend.1 = (bf16[8,128,256]{2,1,0:T(8,128)(2,1)S(1)}, bf16[1024,128]{1,0:T(8,128)(2,1)}) custom-call(s32[8]{0:T(128)S(1)} %and_select_fusion.count, s32[8]{0:T(128)S(1)} %compare_select_fusion.3.seg0, s32[64]{0:T(128)S(1)} %select_reduce_fusion.inv, s32[132,128]{1,0:T(8,128)S(1)} %concatenate.3.code, bf16[8,128,256]{2,1,0:T(8,128)(2,1)S(1)} %get-tuple-element.6.q, ...), custom_call_target="tpu_custom_call" | custom-call | tf_op jit(solution)/shard_map/attend/pallas_call | solution.py:405
  126.2 0.0 slice-done
  126.2 0.0 slice-done.1
  126.2 21.8 %mix.1 = bf16[128,2048]{1,0:T(8,128)(2,1)S(1)} custom-call(bf16[8,128,256]{2,1,0:T(8,128)(2,1)S(1)} %get-tuple-element.8.att, bf16[2048,2048]{1,0:T(8,128)(2,1)S(1)} %bitcast.6), custom_call_target="tpu_custom_call" | custom-call | tf_op jit(solution)/shard_map/mix/pallas_call | solution.py:426
  148.0 0.8 copy.9
  (5 shorter events, 0.0 us)
Async XLA Ops:
  4.8 121.4 %slice-start = ((s8[8388608]{0:T(1024)(128)(4,1)}), s8[4194304]{0:T(1024)(128)(4,1)S(1)}, s32[]{:S(2)}) async-start(s8[8388608]{0:T(1024)(128)(4,1)} %bitcast.5), calls=%async_computation | async-start | bytes 8388608
  4.8 1.2 copy-start
  6.0 120.2 %slice-start.1 = ((s8[8388608]{0:T(1024)(128)(4,1)}), s8[4194304]{0:T(1024)(128)(4,1)S(1)}, s32[]{:S(2)}) async-start(s8[8388608]{0:T(1024)(128)(4,1)} %bitcast.5), calls=%async_computation.1 | async-start | bytes 8388608

commit v2 on v1

--- a/solution.py
+++ b/solution.py
@@ -14,12 +14,13 @@
 QPK = 4
 PAGE = 16
 SEQ = 16
+SEGS = 8
 ROWS = 128
 GT = 1024
 COLS = (QPK + 2) * HD
 STRIPES = 8
 BK = 512
-PAD = BK
+PAD = 3 * BK
 NEG = -1e30
 MESH = pl.DeviceIdType.MESH
 bf16, f32 = jnp.bfloat16, jnp.float32
@@ -207,15 +208,17 @@
         qsends[7].wait_send()
 
 
-def attend(count, seg0, inv, code, q, kv_hbm, att, pool, kv, ve, qe, m, acc, sem, page_sem):
+NT = (((1,), (1,)), ((), ()))
+VR = HD + 16
+
+
+def attend(count, seg0, inv, code, q, kv_hbm, att, pool, kv, kx, vt, qt, m, acc, sa, sb, sem, page_sem):
     s = lax.axis_index("seq")
     chunk = TOKENS // STRIPES
 
     def load(k):
         at = pl.multiple_of(k * chunk, chunk)
-        return pltpu.make_async_copy(
-            kv_hbm.at[pl.ds(at, chunk)], kv.at[pl.ds(pl.multiple_of(PAD + at, 128), chunk)], sem.at[k]
-        )
+        return pltpu.make_async_copy(kv_hbm.at[pl.ds(at, chunk)], kv.at[pl.ds(at, chunk)], sem.at[k])
 
     for k in range(STRIPES):
         load(k).start()
@@ -223,67 +226,92 @@
     @pl.loop(0, TOKENS // PAGE // SEQ)
     def _(i):
         at = pl.multiple_of(inv[i] * PAGE, PAGE)
-        pltpu.make_async_copy(kv_hbm.at[pl.ds(at, PAGE)], pool.at[pl.ds(pl.multiple_of(i * PAGE, PAGE), PAGE)], page_sem).start()
-
-    kv[:PAD] = jnp.zeros((PAD, 2 * HD), bf16)
-    ve[:PAD] = jnp.zeros((PAD, 2 * HD), bf16)
-    low = lax.broadcasted_iota(jnp.int32, (1, 2 * HD), 1) < HD
-    it = lax.broadcasted_iota(jnp.int32, (ROWS, ROWS), 0)
-    iu = lax.broadcasted_iota(jnp.int32, (ROWS, ROWS), 1)
-
-    def scores(c, keys):
-        return lax.dot_general(qe[c], keys, (((1,), (1,)), ((), ())), preferred_element_type=f32)
+        to = pl.multiple_of(i * PAGE, PAGE)
+        pltpu.make_async_copy(kv_hbm.at[pl.ds(at, PAGE)], pool.at[pl.ds(to, PAGE)], page_sem).start()
+
+    down = lax.broadcasted_iota(jnp.int32, (128, 128), 0)
+    along = lax.broadcasted_iota(jnp.int32, (128, 128), 1)
+    eye = (down == along).astype(bf16)
+    pick = (along[:HD] == down[:HD] + HD).astype(bf16)
+    low = along < HD
+    marks = (down >= HD) & (down < HD + SEGS)
+    mark_row = (along[:1] >= HD) & (along[:1] < HD + SEGS)
+    kx[:PAD] = jnp.broadcast_to(jnp.where(mark_row, NEG, 0.0), (PAD, 2 * HD)).astype(bf16)
+    vt[:HD, :PAD] = jnp.zeros((HD, PAD), bf16)
+    vt[HD:, :] = jnp.ones((VR - HD, PAD + TOKENS), bf16)
+
+    def peak(sc):
+        return jnp.max(sc.reshape(sc.shape[0] // 8, 8, sc.shape[1]), axis=0)
+
+    def scores(first):
+        keys = kx[pl.ds(pl.multiple_of(first, 128), BK), :]
+        return jnp.dot(keys, qt[...], preferred_element_type=f32)
 
     @pl.loop(0, STRIPES)
     def _(k):
         load(k).wait()
-
-        @pl.loop(0, chunk // 256)
-        def _(i):
-            at = pl.ds(pl.multiple_of(PAD + k * chunk + i * 256, 256), 256)
-            ve[at] = jnp.where(low, jnp.ones((256, 2 * HD), bf16), kv[at])
-
-        slot = jnp.where(k % 2 == 0, s, 15 - s)
-        stripe = 16 * k + slot
-        t0 = stripe * ROWS
+        at = pl.multiple_of(k * chunk, chunk)
+        rows = kv[pl.ds(at, chunk), :]
+        vt[:HD, pl.ds(pl.multiple_of(PAD + at, 128), chunk)] = lax.dot_general(
+            pick, rows, NT, preferred_element_type=f32
+        ).astype(bf16)
+        for n in range(chunk // 128):
+            row = code[pl.ds(k * (chunk // 128) + n, 1), :]
+            mark = jnp.where(marks & (row != down - HD), NEG, 0.0).astype(bf16)
+            mark = lax.dot_general(eye, mark, NT, preferred_element_type=f32).astype(bf16)
+            to = pl.multiple_of(PAD + at + n * 128, 128)
+            kx[pl.ds(to, 128), :] = jnp.where(low, rows[n * 128 : (n + 1) * 128], mark)
+
+        stripe = 16 * k + jnp.where(k % 2 == 0, s, 15 - s)
         own = seg0[k]
-        zero = jnp.zeros((ROWS, HD), bf16)
-        for c in range(QPK):
-            qe[c] = jnp.concatenate([q[k, :, c * HD : (c + 1) * HD], zero], axis=1)
-
-        here = pl.ds(pl.multiple_of(PAD + t0, 128), ROWS)
-        cu = jnp.broadcast_to(code[pl.ds(PAD // 128 + stripe, 1), :], (ROWS, ROWS))
-        ct = cu.T
-        allowed = ((cu & 15) == (ct & 15)) & (iu <= it) & ((cu < 16) | (iu == it))
-        same = (ct[:, :1] & 15) == own
-        for c in range(QPK):
-            sc = jnp.where(allowed, scores(c, kv[here]), NEG)
-            top = jnp.max(sc, axis=1, keepdims=True)
-            p = jnp.exp(sc - top)
-            acc[c] = jnp.dot(p.astype(bf16), ve[here], preferred_element_type=f32)
-            m[c] = jnp.where(same, top, -NEG)
-
-        @pl.loop(0, count[k])
-        def _(i):
-            first = PAD + t0 - (i + 1) * BK
-            at = pl.ds(pl.multiple_of(first, 128), BK)
-            bias = [
-                jnp.where(code[pl.ds(first // 128 + n, 1), :] == own, 0.0, NEG) for n in range(BK // 128)
-            ]
-            bias = jnp.concatenate(bias, axis=1)
-            for c in range(QPK):
-                sc = scores(c, kv[at]) + bias
-                old = m[c]
-                top = jnp.maximum(old, jnp.max(sc, axis=1, keepdims=True))
-                p = jnp.exp(sc - top)
-                acc[c] = acc[c] * jnp.exp(old - top) + jnp.dot(p.astype(bf16), ve[at], preferred_element_type=f32)
-                m[c] = top
-
+        here = pl.multiple_of(PAD + stripe * ROWS, 128)
         for c in range(0, QPK, 2):
-            a, b = acc[c], acc[c + 1]
-            first_head = pltpu.roll(a, HD, 1) / a
-            second_head = b / pltpu.roll(b, HD, 1)
-            att[k, :, c * HD : (c + 2) * HD] = jnp.where(low, first_head, second_head).astype(bf16)
+            t = q[k, :, c * HD : (c + 2) * HD].T
+            qt[:HD, c * ROWS : (c + 1) * ROWS] = t[:HD]
+            qt[:HD, (c + 1) * ROWS : (c + 2) * ROWS] = t[HD:]
+        qt[HD:, :] = (lax.broadcasted_iota(jnp.int32, (HD, QPK * ROWS), 0) == own).astype(bf16)
+
+        sc = scores(here - BK)
+        sa[...] = sc
+        near = peak(sc)
+
+        row = code[pl.ds(stripe, 1), :]
+        ct = jnp.broadcast_to(row, (ROWS, ROWS))
+        cu = ct.T
+        allowed = ((cu & 15) == (ct & 15)) & (down <= along) & ((cu < 16) | (down == along))
+        same = (row & 15) == own
+        sc = jnp.dot(kx[pl.ds(here, ROWS), :HD], qt[:HD, :], preferred_element_type=f32)
+        sc = jnp.concatenate(
+            [jnp.where(allowed, sc[:, c * ROWS : (c + 1) * ROWS], NEG) for c in range(QPK)], axis=1
+        )
+        top = jnp.max(peak(sc), axis=0, keepdims=True)
+        p = jnp.exp(sc - top).astype(bf16)
+        acc[...] = jnp.dot(vt[:, pl.ds(here, ROWS)], p, preferred_element_type=f32)
+        m[...] = jnp.where(jnp.concatenate([same] * QPK, axis=1), top, -NEG)
+
+        def half(b, src, dst, peaks):
+            first = here - (b + 1) * BK
+            old = m[...]
+            top = jnp.maximum(old, jnp.max(peaks, axis=0, keepdims=True))
+            m[...] = top
+            sc = scores(first - BK)
+            dst[...] = sc
+            p = jnp.exp(src[...] - top).astype(bf16)
+            part = jnp.dot(vt[:, pl.ds(pl.multiple_of(first, 128), BK)], p, preferred_element_type=f32)
+            acc[...] = acc[...] * jnp.exp(old - top) + part
+            return peak(sc)
+
+        def pair(i, peaks):
+            peaks = half(2 * i, sa, sb, peaks)
+            return half(2 * i + 1, sb, sa, peaks)
+
+        lax.fori_loop(0, (count[k] + 1) // 2, pair, near)
+        for c in range(0, QPK, 2):
+            one, two = slice(c * ROWS, (c + 1) * ROWS), slice((c + 1) * ROWS, (c + 2) * ROWS)
+            done = jnp.concatenate(
+                [acc[:HD, one] / acc[HD : HD + 1, one], acc[:HD, two] / acc[HD : HD + 1, two]], axis=0
+            )
+            att[k, :, c * HD : (c + 2) * HD] = done.T.astype(bf16)
 
     pltpu.make_async_copy(kv_hbm.at[pl.ds(0, GT)], pool, page_sem).wait()
 
@@ -400,7 +428,6 @@
         jnp.where(page_table[None, :] == page[:, None], jnp.arange(TOKENS // PAGE, dtype=jnp.int32)[None, :], 0), axis=1
     )
     code = (seg_ids + 16 * (1 - live)).reshape(TOKENS // 128, 128)
-    code = jnp.concatenate([jnp.full((PAD // 128, 128), 255, jnp.int32), code], axis=0)
 
     att, pool = pl.pallas_call(
         attend,
@@ -411,11 +438,14 @@
         in_specs=[SMEM, SMEM, SMEM, VMEM, VMEM, ANY],
         out_specs=(VMEM, ANY),
         scratch_shapes=[
+            pltpu.VMEM((TOKENS, 2 * HD), bf16),
             pltpu.VMEM((PAD + TOKENS, 2 * HD), bf16),
-            pltpu.VMEM((PAD + TOKENS, 2 * HD), bf16),
-            pltpu.VMEM((QPK, ROWS, 2 * HD), bf16),
-            pltpu.VMEM((QPK, ROWS, 1), f32),
-            pltpu.VMEM((QPK, ROWS, 2 * HD), f32),
+            pltpu.VMEM((VR, PAD + TOKENS), bf16),
+            pltpu.VMEM((2 * HD, QPK * ROWS), bf16),
+            pltpu.VMEM((1, QPK * ROWS), f32),
+            pltpu.VMEM((VR, QPK * ROWS), f32),
+            pltpu.VMEM((BK, QPK * ROWS), f32),
+            pltpu.VMEM((BK, QPK * ROWS), f32),
             DMA((STRIPES,)),
             DMA,
         ],

time: 149 us -> 102 us (0.68)
  Pallas kernels: 142 us -> 94.7 us
    pallas_call x1, Pallas kernels: 75.3 us -> 27.1 us  [shards(): pl.pallas_call(attend, out_shape=(jax.ShapeDtypeStruct((STRIPES, ROWS, QP...]
where the time goes in v2:
time: 102 us
  Pallas kernels  94.7 us (93%)
  local copies, waits for them, and re-layouts  3.26 us (3%)
  other arithmetic  3.11 us (3%)
    pallas_call x1, Pallas kernels, shards(): pl.pallas_call(project, out_shape=(jax.ShapeDtypeStruct((STRIPES, ROWS, Q...  44.9 us
    pallas_call x1, Pallas kernels, shards(): pl.pallas_call(attend, out_shape=(jax.ShapeDtypeStruct((STRIPES, ROWS, QP...  27.1 us
    pallas_call x1, Pallas kernels, shards(): pl.pallas_call(mix, out_shape=jax.ShapeDtypeStruct((ROWS, D), bf16), in_s...  22.7 us
    unnamed x7, local copies, waits for them, and re-layouts  2.1 us

profile of v2, /device:TPU:5, one launch (start us, length us, event | category | flops | bytes accessed | tf_op | source)
XLA Modules:
  0.0 101.8 jit_solution(12102321156662778005)
XLA Ops:
  0.6 0.9 select_reduce_fusion.inv
  1.5 1.2 %dynamic-slice_reduce_fusion = (s32[8]{0:T(128)S(1)}, s32[8]{0:T(128)S(1)}) fusion(s32[8,16,1]{2,1,0:T(8,128)} %bitcast.7, s32[]{:T(128)S(6)} %select_n.38, s32[]{:T(128)S(6)} %select_n.37), kind=kLoop, calls=%fused_computation.3 | loop fusion | bytes 136 | tf_op jit(solution)/shard_map/dynamic_slice | solution.py:419
  2.7 1.2 %convert_reduce_fusion = s32[8]{0:T(128)S(1)} fusion(s32[16384]{0:T(1024)} %param.9, s32[8]{0:T(128)S(1)} %compare_select_fusion.3.seg0), kind=kLoop, calls=%fused_computation | loop fusion | flops 393208 | bytes 65600 | tf_op jit(solution)/shard_map/reduce_sum | solution.py:423
  3.9 0.0 slice-start
  3.9 1.0 %add_bitcast_fusion.code = s32[128,128]{1,0:T(8,128)S(1)} fusion(s32[16384]{0:T(1024)} %param.9, s32[16384]{0:T(1024)} %param.10), kind=kLoop, calls=%fused_computation.2 | loop fusion | flops 49152 | bytes 196608 | tf_op jit(solution)/shard_map/reshape | solution.py:430
  4.9 0.0 copy-start
  4.9 1.3 %copy-done = bf16[128,2048]{1,0:T(8,128)(2,1)S(1)} copy-done((bf16[128,2048]{1,0:T(8,128)(2,1)S(1)}, bf16[128,2048]{1,0:T(8,128)(2,1)}, u32[]{:S(2)}) %copy-start) | copy-done | bytes 524312
  6.2 0.0 slice-start.1
  6.2 44.9 %project.1 = (bf16[8,128,256]{2,1,0:T(8,128)(2,1)S(1)}, bf16[16384,128]{1,0:T(8,128)(2,1)S(1)}) custom-call(bf16[128,2048]{1,0:T(8,128)(2,1)S(1)} %copy-done, bf16[2048,3072]{1,0:T(8,128)(2,1)} %w.2), custom_call_target="tpu_custom_call" | custom-call | tf_op jit(solution)/shard_map/project/pallas_call | solution.py:390
  51.1 27.1 %attend.1 = (bf16[8,128,256]{2,1,0:T(8,128)(2,1)S(1)}, bf16[1024,128]{1,0:T(8,128)(2,1)}) custom-call(s32[8]{0:T(128)S(1)} %and_select_fusion.count, s32[8]{0:T(128)S(1)} %compare_select_fusion.3.seg0, s32[64]{0:T(128)S(1)} %select_reduce_fusion.inv, s32[128,128]{1,0:T(8,128)S(1)} %add_bitcast_fusion.code, bf16[8,128,256]{2,1,0:T(8,128)(2,1)S(1)} %get-tuple-element.6.q, ...), custom_call_target="tpu_custom_call" | custom-call | tf_op jit(solution)/shard_map/attend/pallas_call | solution.py:432
  78.2 0.0 slice-done
  78.2 0.0 slice-done.1
  78.3 22.7 %mix.1 = bf16[128,2048]{1,0:T(8,128)(2,1)S(1)} custom-call(bf16[8,128,256]{2,1,0:T(8,128)(2,1)S(1)} %get-tuple-element.8.att, bf16[2048,2048]{1,0:T(8,128)(2,1)S(1)} %bitcast.6), custom_call_target="tpu_custom_call" | custom-call | tf_op jit(solution)/shard_map/mix/pallas_call | solution.py:456
  101.0 0.8 copy.9
  (4 shorter events, 0.0 us)
Async XLA Ops:
  3.9 74.4 %slice-start = ((s8[8388608]{0:T(1024)(128)(4,1)}), s8[4194304]{0:T(1024)(128)(4,1)S(1)}, s32[]{:S(2)}) async-start(s8[8388608]{0:T(1024)(128)(4,1)} %bitcast.5), calls=%async_computation | async-start | bytes 8388608
  4.9 1.3 %copy-start = (bf16[128,2048]{1,0:T(8,128)(2,1)S(1)}, bf16[128,2048]{1,0:T(8,128)(2,1)}, u32[]{:S(2)}) copy-start(bf16[128,2048]{1,0:T(8,128)(2,1)} %hid.1) | copy-start | bytes 1572868
  6.2 72.0 %slice-start.1 = ((s8[8388608]{0:T(1024)(128)(4,1)}), s8[4194304]{0:T(1024)(128)(4,1)S(1)}, s32[]{:S(2)}) async-start(s8[8388608]{0:T(1024)(128)(4,1)} %bitcast.5), calls=%async_computation.1 | async-start | bytes 8388608

commit v3 on v2

--- a/solution.py
+++ b/solution.py
@@ -21,18 +21,31 @@
 STRIPES = 8
 BK = 512
 PAD = 3 * BK
+EARLY = 3
 NEG = -1e30
 MESH = pl.DeviceIdType.MESH
 bf16, f32 = jnp.bfloat16, jnp.float32
 
 
+MASKS = (0, 11, 13, 6)
+
+
+def flip(value, x):
+    if isinstance(x, int):
+        bits = [(MASKS[x] >> n) % 2 for n in range(4)]
+    else:
+        low, high = x % 2, x // 2
+        both = (low + high) % 2
+        bits = [both, low, high, both]
+    return sum(((value // (1 << n) + bits[n]) % 2) * (1 << n) for n in range(4))
+
+
 def dealt(s, j):
-    slot = (s % 2) * 8 + j
-    return jnp.where((s // 2) % 2 == 0, slot, 15 - slot)
+    return flip((s % 2) * 8 + j, (s // 2) % 4)
 
 
 def held(s, k):
-    slot = s if k % 2 == 0 else 15 - s
+    slot = flip(s, k % 4)
     return 2 * k + slot // 8, slot % 8
 
 
@@ -85,7 +98,6 @@
         kvs[r] = jnp.dot(hv[...], wk[r], preferred_element_type=f32).astype(bf16)
         if r == 0:
             pl.semaphore_wait(barrier, jnp.where(mine, 18, 19))
-
         if r < 7:
             cp = pltpu.make_async_remote_copy(
                 src_ref=kvs.at[r],
@@ -101,18 +113,46 @@
             own_kv = pltpu.make_async_copy(kvs.at[r], kv_out.at[pl.ds(row0, ROWS)], loc)
             own_kv.start()
 
+    H = GT // 2
+    R, L, Z, C = range(4)
+
+    def half(b, h):
+        return kv_out.at[pl.ds(pl.multiple_of(b * GT + h * H, 128), H)]
+
+    count = [0]
+
+    def pass_on(b, h, *to_peers):
+        for peer in to_peers:
+            i = count[0]
+            count[0] += 1
+            cp = pltpu.make_async_remote_copy(
+                src_ref=half(b, h),
+                dst_ref=half(b, h),
+                send_sem=g_s.at[i],
+                recv_sem=g_r.at[i],
+                device_id=peers[peer],
+                device_id_type=MESH,
+            )
+            cp.start()
+            sends.append(cp)
+
+    def arrived(b, h, i):
+        pltpu.make_async_copy(half(b, h), half(b, h), g_r.at[i]).wait()
+
     slot = s // 2
     qsends = []
-    for r in range(8):
-        g = lax.rem(j + r + 1, 8)
+
+    def query(r):
         loads[8 + r].wait()
         qs[r] = (jnp.dot(hv[...], wq[r], preferred_element_type=f32).astype(bf16) * 0.015625).astype(bf16)
+
+    def send_query(r):
         cp = pltpu.make_async_remote_copy(
             src_ref=qs.at[r],
             dst_ref=q_out.at[slot],
             send_sem=q_s.at[r],
             recv_sem=q_r.at[slot],
-            device_id=(to, g),
+            device_id=(to, lax.rem(j + r + 1, 8)),
             device_id_type=MESH,
         )
         qsends.append(cp)
@@ -128,75 +168,66 @@
             def _():
                 pltpu.make_async_copy(qs.at[7], q_out.at[slot], q_r.at[slot]).start()
 
-    def rows(b, first_row, count):
-        return kv_out.at[pl.ds(pl.multiple_of(b * GT + first_row, 128), count)]
-
-    def arrived(b, first_row, count, i):
-        there = rows(b, first_row, count)
-        pltpu.make_async_copy(there, there, g_r.at[i]).wait()
-
-    def pass_on(b, first_row, count, i, peer):
-        there = rows(b, first_row, count)
-        cp = pltpu.make_async_remote_copy(
-            src_ref=there,
-            dst_ref=there,
-            send_sem=g_s.at[i],
-            recv_sem=g_r.at[i],
-            device_id=peers[peer],
-            device_id_type=MESH,
-        )
-        cp.start()
-        sends.append(cp)
-
-    R, L, Z, C = range(4)
+    for r in range(EARLY):
+        query(r)
     own_kv.wait()
     for r in range(7):
         source = lax.rem(j + 7 - r, 8)
         there = kv_out.at[pl.ds(pl.multiple_of(s * GT + source * ROWS, ROWS), ROWS)]
         pltpu.make_async_copy(there, there, a2a_r.at[r]).wait()
-    H = GT // 2
     me = block(zh, x, c)
-    pass_on(me, 0, GT, 0, R)
-    pass_on(me, 0, GT, 1, L)
-    pass_on(me, 0, GT, 2, Z)
-    pass_on(me, 0, GT, 3, C)
     bl, br, bf = block(zh, left, c), block(zh, right, c), block(zh, far, c)
     zm, zl, zr, zf = block(1 - zh, x, c), block(1 - zh, left, c), block(1 - zh, right, c), block(1 - zh, far, c)
-    arrived(bl, 0, GT, 0)
-    pass_on(bl, 0, H, 4, R)
-    pass_on(bl, 0, GT, 6, C)
-    arrived(br, 0, GT, 1)
-    pass_on(br, H, H, 5, L)
-    pass_on(br, 0, GT, 7, C)
-    arrived(zm, 0, GT, 2)
-    pass_on(zm, 0, GT, 10, R)
-    pass_on(zm, 0, GT, 11, L)
-    pass_on(zm, 0, GT, 12, C)
-    arrived(bf, 0, H, 4)
-    pass_on(bf, 0, H, 8, C)
-    arrived(bf, H, H, 5)
-    pass_on(bf, H, H, 9, C)
-    arrived(zl, 0, GT, 10)
-    pass_on(zl, 0, H, 13, R)
-    pass_on(zl, 0, GT, 15, C)
-    arrived(zr, 0, GT, 11)
-    pass_on(zr, H, H, 14, L)
-    pass_on(zr, 0, GT, 16, C)
-    arrived(zf, 0, H, 13)
-    pass_on(zf, 0, H, 17, C)
-    arrived(zf, H, H, 14)
-    pass_on(zf, H, H, 18, C)
+    pass_on(me, 0, R, Z)
+    pass_on(me, 1, L, Z)
+    pass_on(me, 1, R)
+    pass_on(me, 0, L, C)
+    pass_on(me, 1, C)
+    for r in range(EARLY, 8):
+        query(r)
+    for r in range(8):
+        send_query(r)
+    arrived(bl, 0, 0)
+    pass_on(bl, 0, R, C)
+    arrived(br, 1, 2)
+    pass_on(br, 1, L, C)
+    arrived(zm, 0, 1)
+    pass_on(zm, 0, R, L, C)
+    arrived(zm, 1, 3)
+    pass_on(zm, 1, R, L, C)
+    arrived(bl, 1, 4)
+    pass_on(bl, 1, C)
+    arrived(br, 0, 5)
+    pass_on(br, 0, C)
+    arrived(bf, 0, 8)
+    pass_on(bf, 0, Z, C)
+    arrived(bf, 1, 10)
+    pass_on(bf, 1, Z, C)
+    arrived(zl, 0, 12)
+    pass_on(zl, 0, C)
+    arrived(zr, 0, 13)
+    pass_on(zr, 0, C)
+    arrived(zl, 1, 15)
+    pass_on(zl, 1, C)
+    arrived(zr, 1, 16)
+    pass_on(zr, 1, C)
+    arrived(zf, 0, 20)
+    pass_on(zf, 0, C)
+    arrived(zf, 1, 22)
+    pass_on(zf, 1, C)
     d = 1 - c
-    arrived(block(zh, x, d), 0, GT, 3)
-    arrived(block(zh, left, d), 0, GT, 6)
-    arrived(block(zh, right, d), 0, GT, 7)
-    arrived(block(zh, far, d), 0, H, 8)
-    arrived(block(zh, far, d), H, H, 9)
-    arrived(block(1 - zh, x, d), 0, GT, 12)
-    arrived(block(1 - zh, left, d), 0, GT, 15)
-    arrived(block(1 - zh, right, d), 0, GT, 16)
-    arrived(block(1 - zh, far, d), 0, H, 17)
-    arrived(block(1 - zh, far, d), H, H, 18)
+    for zz, xx, first, second in (
+        (zh, x, 6, 7),
+        (zh, left, 9, 18),
+        (zh, right, 19, 11),
+        (zh, far, 21, 23),
+        (1 - zh, x, 14, 17),
+        (1 - zh, left, 24, 26),
+        (1 - zh, right, 25, 27),
+        (1 - zh, far, 28, 29),
+    ):
+        arrived(block(zz, xx, d), 0, first)
+        arrived(block(zz, xx, d), 1, second)
 
     for k in range(STRIPES):
         pltpu.make_async_copy(q_out.at[k], q_out.at[k], q_r.at[k]).wait()
@@ -262,7 +293,7 @@
             to = pl.multiple_of(PAD + at + n * 128, 128)
             kx[pl.ds(to, 128), :] = jnp.where(low, rows[n * 128 : (n + 1) * 128], mark)
 
-        stripe = 16 * k + jnp.where(k % 2 == 0, s, 15 - s)
+        stripe = 16 * k + flip(s, k % 4)
         own = seg0[k]
         here = pl.multiple_of(PAD + stripe * ROWS, 128)
         for c in range(0, QPK, 2):
@@ -406,8 +437,8 @@
             DMA((7,)),
             DMA((8,)),
             DMA((8,)),
-            DMA((19,)),
-            DMA((19,)),
+            DMA((30,)),
+            DMA((30,)),
             DMA,
         ],
         compiler_params=pltpu.CompilerParams(collective_id=0, has_side_effects=True, vmem_limit_bytes=40 << 20),
@@ -415,13 +446,11 @@
     )(hidden, w_qkv)
 
     heads = seg_ids.reshape(STRIPES, SEQ, ROWS)[:, :, 0]
-    even = lax.dynamic_slice_in_dim(heads, s, 1, 1)[:, 0]
-    odd = lax.dynamic_slice_in_dim(heads, 15 - s, 1, 1)[:, 0]
     number = jnp.arange(STRIPES, dtype=jnp.int32)
-    is_even = number % 2 == 0
-    seg0 = jnp.where(is_even, even, odd)
+    slots = flip(s, number % 4)
+    seg0 = jnp.sum(jnp.where(jnp.arange(SEQ, dtype=jnp.int32)[None, :] == slots[:, None], heads, 0), axis=1)
     begin = jnp.sum((seg_ids[None, :] < seg0[:, None]).astype(jnp.int32), axis=1)
-    t0 = (16 * number + jnp.where(is_even, s, 15 - s)) * ROWS
+    t0 = (16 * number + slots) * ROWS
     count = (t0 - begin + BK - 1) // BK
     page = s * (TOKENS // PAGE // SEQ) + jnp.arange(TOKENS // PAGE // SEQ, dtype=jnp.int32)
     inv = jnp.sum(

time: 102 us -> 98.9 us (0.970)
  the two profiles are of different devices: /device:TPU:5 before, /device:TPU:1 now
where the time goes in v3:
time: 98.9 us; the launch traced here: 98.7 us
  Pallas kernels  91.5 us (93%)
  other arithmetic  3.33 us (3%)
  local copies, waits for them, and re-layouts  3.15 us (3%)
    pallas_call x1, Pallas kernels, shards(): pl.pallas_call(project, out_shape=(jax.ShapeDtypeStruct((STRIPES, ROWS, Q...  39.8 us
    pallas_call x1, Pallas kernels, shards(): pl.pallas_call(attend, out_shape=(jax.ShapeDtypeStruct((STRIPES, ROWS, QP...  26.4 us
    pallas_call x1, Pallas kernels, shards(): pl.pallas_call(mix, out_shape=jax.ShapeDtypeStruct((ROWS, D), bf16), in_s...  25.2 us
    unnamed x7, local copies, waits for them, and re-layouts  2.1 us

profile of v3, /device:TPU:1, one launch (start us, length us, event | category | flops | bytes accessed | tf_op | source)
XLA Modules:
  0.0 98.7 jit_solution(4458104870376056979)
XLA Ops:
  0.7 0.9 select_reduce_fusion.inv
  1.6 1.0 %slice_reduce_fusion = s32[8,16]{1,0:T(8,128)S(1)} fusion(s32[8,16,128]{2,1,0:T(8,128)} %bitcast.6), kind=kLoop, calls=%fused_computation.2 | loop fusion | bytes 1024 | tf_op jit(solution)/shard_map/slice | solution.py:448
  2.7 0.2 select_reduce_fusion.1.seg0
  2.8 1.2 %convert_reduce_fusion = s32[8]{0:T(128)S(1)} fusion(s32[16384]{0:T(1024)} %param.9, s32[8]{0:T(128)S(1)} %select_reduce_fusion.1.seg0), kind=kLoop, calls=%fused_computation | loop fusion | flops 393208 | bytes 65600 | tf_op jit(solution)/shard_map/reduce_sum | solution.py:452
  4.0 0.0 slice-start
  4.0 1.0 %add_bitcast_fusion.code = s32[128,128]{1,0:T(8,128)S(1)} fusion(s32[16384]{0:T(1024)} %param.9, s32[16384]{0:T(1024)} %param.10), kind=kLoop, calls=%fused_computation.3 | loop fusion | flops 49152 | bytes 196608 | tf_op jit(solution)/shard_map/reshape | solution.py:459
  5.1 0.0 copy-start
  5.1 1.3 %copy-done = bf16[128,2048]{1,0:T(8,128)(2,1)S(1)} copy-done((bf16[128,2048]{1,0:T(8,128)(2,1)S(1)}, bf16[128,2048]{1,0:T(8,128)(2,1)}, u32[]{:S(2)}) %copy-start) | copy-done | bytes 524312
  6.4 0.0 slice-start.1
  6.4 39.8 %project.1 = (bf16[8,128,256]{2,1,0:T(8,128)(2,1)S(1)}, bf16[16384,128]{1,0:T(8,128)(2,1)S(1)}) custom-call(bf16[128,2048]{1,0:T(8,128)(2,1)S(1)} %copy-done, bf16[2048,3072]{1,0:T(8,128)(2,1)} %w.2), custom_call_target="tpu_custom_call" | custom-call | tf_op jit(solution)/shard_map/project/pallas_call | solution.py:421
  46.2 26.4 %attend.1 = (bf16[8,128,256]{2,1,0:T(8,128)(2,1)S(1)}, bf16[1024,128]{1,0:T(8,128)(2,1)}) custom-call(s32[8]{0:T(128)S(1)} %and_select_fusion.count, s32[8]{0:T(128)S(1)} %select_reduce_fusion.1.seg0, s32[64]{0:T(128)S(1)} %select_reduce_fusion.inv, s32[128,128]{1,0:T(8,128)S(1)} %add_bitcast_fusion.code, bf16[8,128,256]{2,1,0:T(8,128)(2,1)S(1)} %get-tuple-element.6.q, ...), custom_call_target="tpu_custom_call" | custom-call | tf_op jit(solution)/shard_map/attend/pallas_call | solution.py:461
  72.6 0.0 slice-done
  72.6 0.0 slice-done.1
  72.7 25.2 %mix.1 = bf16[128,2048]{1,0:T(8,128)(2,1)S(1)} custom-call(bf16[8,128,256]{2,1,0:T(8,128)(2,1)S(1)} %get-tuple-element.8.att, bf16[2048,2048]{1,0:T(8,128)(2,1)S(1)} %bitcast.5), custom_call_target="tpu_custom_call" | custom-call | tf_op jit(solution)/shard_map/mix/pallas_call | solution.py:485
  97.9 0.8 copy.9
  (4 shorter events, 0.1 us)
Async XLA Ops:
  4.0 68.6 %slice-start = ((s8[8388608]{0:T(1024)(128)(4,1)}), s8[4194304]{0:T(1024)(128)(4,1)S(1)}, s32[]{:S(2)}) async-start(s8[8388608]{0:T(1024)(128)(4,1)} %bitcast.4), calls=%async_computation | async-start | bytes 8388608
  5.1 1.3 %copy-start = (bf16[128,2048]{1,0:T(8,128)(2,1)S(1)}, bf16[128,2048]{1,0:T(8,128)(2,1)}, u32[]{:S(2)}) copy-start(bf16[128,2048]{1,0:T(8,128)(2,1)} %hid.1) | copy-start | bytes 1572868
  6.4 66.3 %slice-start.1 = ((s8[8388608]{0:T(1024)(128)(4,1)}), s8[4194304]{0:T(1024)(128)(4,1)S(1)}, s32[]{:S(2)}) async-start(s8[8388608]{0:T(1024)(128)(4,1)} %bitcast.4), calls=%async_computation.1 | async-start | bytes 8388608

commit v4 on v3

--- a/solution.py
+++ b/solution.py
@@ -20,7 +20,8 @@
 COLS = (QPK + 2) * HD
 STRIPES = 8
 BK = 512
-PAD = 3 * BK
+PAD = 2 * BK
+META = STRIPES + 64
 EARLY = 3
 NEG = -1e30
 MESH = pl.DeviceIdType.MESH
@@ -28,6 +29,10 @@
 
 
 MASKS = (0, 11, 13, 6)
+
+
+NT = (((1,), (1,)), ((), ()))
+VR = HD + 16
 
 
 def flip(value, x):
@@ -49,14 +54,15 @@
     return 2 * k + slot // 8, slot % 8
 
 
-def project(hid, w, q_out, kv_out, hv, wk, wq, kvs, qs, load, a2a_s, a2a_r, q_s, q_r, g_s, g_r, loc):
+def project(
+    hv, w, seg, live, table, q_out, kv_out, kx, vt, code, meta,
+    wk, wq, kvs, qs, load, a2a_s, a2a_r, q_s, q_r, g_s, g_r, loc,
+):
     s, j = lax.axis_index("seq"), lax.axis_index("head")
     zh, x, c = s // 8, (s // 2) % 4, s % 2
     to = dealt(s, j)
     mine = to == s
 
-    first = pltpu.make_async_copy(hid, hv, load.at[16])
-    first.start()
     loads = []
     for r in range(8):
         g = lax.rem(j + r + 1, 8)
@@ -67,7 +73,6 @@
         g = lax.rem(j + r + 1, 8)
         col = pl.multiple_of(g * COLS, 128)
         loads.append(pltpu.make_async_copy(w.at[:, pl.ds(col, QPK * HD)], wq.at[r], load.at[8 + r]))
-        loads[-1].start()
 
     def block(zz, xx, cc):
         return zz * 8 + xx * 2 + cc
@@ -88,7 +93,48 @@
         def _():
             pl.semaphore_signal(barrier, inc=1, device_id=held(s, k), device_id_type=MESH)
 
-    first.wait()
+    down = lax.broadcasted_iota(jnp.int32, (128, 128), 0)
+    along = lax.broadcasted_iota(jnp.int32, (128, 128), 1)
+    eye = (down == along).astype(bf16)
+    pick = (along[:HD] == down[:HD] + HD).astype(bf16)
+    marks = (down >= HD) & (down < HD + SEGS)
+    mark_row = (along[:1] >= HD) & (along[:1] < HD + SEGS)
+
+    def tables():
+        code[...] = seg[...] + 16 * (1 - live[...])
+        lane = along[:1]
+        for k in range(STRIPES):
+            stripe = 16 * k + flip(s, k % 4)
+            own = seg[pl.ds(stripe, 1), :][:, :1]
+            before = jnp.where(seg[...] < own, 1.0, 0.0)
+            begin = jnp.sum(jnp.sum(before, axis=0, keepdims=True), axis=1, keepdims=True).astype(jnp.int32)
+            blocks = lax.shift_right_logical(stripe * ROWS - begin + BK - 1, BK.bit_length() - 1)
+            meta[k : k + 1, :] = jnp.where(lane == 0, blocks, own)
+        at = jnp.zeros((64, 128), f32)
+        for n in range(TOKENS // PAGE // 128):
+            hit = table[n : n + 1, :] == 64 * s + down[:64]
+            at += jnp.where(hit, (n * 128 + along[:64]).astype(f32), 0.0)
+        logical = jnp.sum(at, axis=1, keepdims=True).astype(jnp.int32)
+        meta[STRIPES:, :] = jnp.broadcast_to(logical, (64, 128))
+        kx[:PAD] = jnp.broadcast_to(jnp.where(mark_row, NEG, 0.0), (PAD, 2 * HD)).astype(bf16)
+        vt[:HD, :PAD] = jnp.zeros((HD, PAD), bf16)
+        vt[HD:, :] = jnp.ones((VR - HD, PAD + TOKENS), bf16)
+
+    def mark_keys(first, stop):
+        @pl.loop(first, stop)
+        def _(i):
+            for n in range(8):
+                row = code[pl.ds(i * 8 + n, 1), :]
+                mark = jnp.where(marks & (row != down - HD), NEG, 0.0).astype(bf16)
+                mark = lax.dot_general(eye, mark, NT, preferred_element_type=f32).astype(bf16)
+                kx[pl.ds(pl.multiple_of(PAD + (i * 8 + n) * 128, 128), 128), :] = mark
+
+    def use(b, h):
+        at = pl.multiple_of(b * GT + h * (GT // 2), 128)
+        to = pl.multiple_of(PAD + at, 128)
+        rows = kv_out[pl.ds(at, GT // 2), :]
+        vt[:HD, pl.ds(to, GT // 2)] = lax.dot_general(pick, rows, NT, preferred_element_type=f32).astype(bf16)
+        kx[pl.ds(to, GT // 2), :] = jnp.where(along[:1] < HD, rows, kx[pl.ds(to, GT // 2), :])
 
     row0 = pl.multiple_of(s * GT + j * ROWS, ROWS)
     sends = []
@@ -168,6 +214,10 @@
             def _():
                 pltpu.make_async_copy(qs.at[7], q_out.at[slot], q_r.at[slot]).start()
 
+    for r in range(8):
+        loads[8 + r].start()
+    tables()
+    mark_keys(0, 8)
     for r in range(EARLY):
         query(r)
     own_kv.wait()
@@ -187,47 +237,75 @@
         query(r)
     for r in range(8):
         send_query(r)
+    mark_keys(8, 16)
+    d = 1 - c
+    ome, ol, or_, of = block(zh, x, d), block(zh, left, d), block(zh, right, d), block(zh, far, d)
+    oz, ozl, ozr, ozf = block(1 - zh, x, d), block(1 - zh, left, d), block(1 - zh, right, d), block(1 - zh, far, d)
     arrived(bl, 0, 0)
     pass_on(bl, 0, R, C)
     arrived(br, 1, 2)
     pass_on(br, 1, L, C)
     arrived(zm, 0, 1)
     pass_on(zm, 0, R, L, C)
+    use(me, 0)
+    use(me, 1)
     arrived(zm, 1, 3)
     pass_on(zm, 1, R, L, C)
     arrived(bl, 1, 4)
     pass_on(bl, 1, C)
     arrived(br, 0, 5)
     pass_on(br, 0, C)
+    use(bl, 0)
+    use(br, 1)
     arrived(bf, 0, 8)
     pass_on(bf, 0, Z, C)
     arrived(bf, 1, 10)
     pass_on(bf, 1, Z, C)
+
+    def other(b, h, i):
+        arrived(b, h, i)
+        use(b, h)
+
+    use(zm, 0)
+    use(zm, 1)
+    use(bl, 1)
+    use(br, 0)
+    other(ome, 0, 6)
+    other(ome, 1, 7)
+    other(ol, 0, 9)
+    other(or_, 1, 11)
+    other(oz, 0, 14)
     arrived(zl, 0, 12)
     pass_on(zl, 0, C)
     arrived(zr, 0, 13)
     pass_on(zr, 0, C)
+    other(oz, 1, 17)
+    other(ol, 1, 18)
+    other(or_, 0, 19)
+    use(bf, 0)
+    use(bf, 1)
+    other(of, 0, 21)
+    other(of, 1, 23)
+    arrived(zf, 0, 20)
+    pass_on(zf, 0, C)
+    use(zl, 0)
+    use(zr, 0)
     arrived(zl, 1, 15)
     pass_on(zl, 1, C)
     arrived(zr, 1, 16)
     pass_on(zr, 1, C)
-    arrived(zf, 0, 20)
-    pass_on(zf, 0, C)
     arrived(zf, 1, 22)
     pass_on(zf, 1, C)
-    d = 1 - c
-    for zz, xx, first, second in (
-        (zh, x, 6, 7),
-        (zh, left, 9, 18),
-        (zh, right, 19, 11),
-        (zh, far, 21, 23),
-        (1 - zh, x, 14, 17),
-        (1 - zh, left, 24, 26),
-        (1 - zh, right, 25, 27),
-        (1 - zh, far, 28, 29),
-    ):
-        arrived(block(zz, xx, d), 0, first)
-        arrived(block(zz, xx, d), 1, second)
+    use(zf, 0)
+    other(ozl, 0, 24)
+    other(ozr, 0, 25)
+    use(zl, 1)
+    use(zr, 1)
+    other(ozf, 0, 26)
+    use(zf, 1)
+    other(ozl, 1, 27)
+    other(ozr, 1, 28)
+    other(ozf, 1, 29)
 
     for k in range(STRIPES):
         pltpu.make_async_copy(q_out.at[k], q_out.at[k], q_r.at[k]).wait()
@@ -239,37 +317,12 @@
         qsends[7].wait_send()
 
 
-NT = (((1,), (1,)), ((), ()))
-VR = HD + 16
-
-
-def attend(count, seg0, inv, code, q, kv_hbm, att, pool, kv, kx, vt, qt, m, acc, sa, sb, sem, page_sem):
+def attend(meta_in, code, q, kv, kx, vt, att, pool, meta, qt, m, acc, sa, sb, sem, page_sem):
     s = lax.axis_index("seq")
-    chunk = TOKENS // STRIPES
-
-    def load(k):
-        at = pl.multiple_of(k * chunk, chunk)
-        return pltpu.make_async_copy(kv_hbm.at[pl.ds(at, chunk)], kv.at[pl.ds(at, chunk)], sem.at[k])
-
-    for k in range(STRIPES):
-        load(k).start()
-
-    @pl.loop(0, TOKENS // PAGE // SEQ)
-    def _(i):
-        at = pl.multiple_of(inv[i] * PAGE, PAGE)
-        to = pl.multiple_of(i * PAGE, PAGE)
-        pltpu.make_async_copy(kv_hbm.at[pl.ds(at, PAGE)], pool.at[pl.ds(to, PAGE)], page_sem).start()
-
+    fetch = pltpu.make_async_copy(meta_in, meta, sem)
+    fetch.start()
     down = lax.broadcasted_iota(jnp.int32, (128, 128), 0)
     along = lax.broadcasted_iota(jnp.int32, (128, 128), 1)
-    eye = (down == along).astype(bf16)
-    pick = (along[:HD] == down[:HD] + HD).astype(bf16)
-    low = along < HD
-    marks = (down >= HD) & (down < HD + SEGS)
-    mark_row = (along[:1] >= HD) & (along[:1] < HD + SEGS)
-    kx[:PAD] = jnp.broadcast_to(jnp.where(mark_row, NEG, 0.0), (PAD, 2 * HD)).astype(bf16)
-    vt[:HD, :PAD] = jnp.zeros((HD, PAD), bf16)
-    vt[HD:, :] = jnp.ones((VR - HD, PAD + TOKENS), bf16)
 
     def peak(sc):
         return jnp.max(sc.reshape(sc.shape[0] // 8, 8, sc.shape[1]), axis=0)
@@ -278,23 +331,18 @@
         keys = kx[pl.ds(pl.multiple_of(first, 128), BK), :]
         return jnp.dot(keys, qt[...], preferred_element_type=f32)
 
+    fetch.wait()
+
+    @pl.loop(0, TOKENS // PAGE // SEQ)
+    def _(i):
+        at = pl.multiple_of(meta[STRIPES + i, 0] * PAGE, PAGE)
+        to = pl.multiple_of(i * PAGE, PAGE)
+        pltpu.make_async_copy(kv.at[pl.ds(at, PAGE)], pool.at[pl.ds(to, PAGE)], page_sem).start()
+
     @pl.loop(0, STRIPES)
     def _(k):
-        load(k).wait()
-        at = pl.multiple_of(k * chunk, chunk)
-        rows = kv[pl.ds(at, chunk), :]
-        vt[:HD, pl.ds(pl.multiple_of(PAD + at, 128), chunk)] = lax.dot_general(
-            pick, rows, NT, preferred_element_type=f32
-        ).astype(bf16)
-        for n in range(chunk // 128):
-            row = code[pl.ds(k * (chunk // 128) + n, 1), :]
-            mark = jnp.where(marks & (row != down - HD), NEG, 0.0).astype(bf16)
-            mark = lax.dot_general(eye, mark, NT, preferred_element_type=f32).astype(bf16)
-            to = pl.multiple_of(PAD + at + n * 128, 128)
-            kx[pl.ds(to, 128), :] = jnp.where(low, rows[n * 128 : (n + 1) * 128], mark)
-
         stripe = 16 * k + flip(s, k % 4)
-        own = seg0[k]
+        own = meta[k, 1]
         here = pl.multiple_of(PAD + stripe * ROWS, 128)
         for c in range(0, QPK, 2):
             t = q[k, :, c * HD : (c + 2) * HD].T
@@ -320,23 +368,30 @@
         acc[...] = jnp.dot(vt[:, pl.ds(here, ROWS)], p, preferred_element_type=f32)
         m[...] = jnp.where(jnp.concatenate([same] * QPK, axis=1), top, -NEG)
 
-        def half(b, src, dst, peaks):
+        def weigh(b, src, peaks, dst=None):
             first = here - (b + 1) * BK
             old = m[...]
             top = jnp.maximum(old, jnp.max(peaks, axis=0, keepdims=True))
             m[...] = top
-            sc = scores(first - BK)
-            dst[...] = sc
+            if dst is not None:
+                sc = scores(first - BK)
+                dst[...] = sc
             p = jnp.exp(src[...] - top).astype(bf16)
             part = jnp.dot(vt[:, pl.ds(pl.multiple_of(first, 128), BK)], p, preferred_element_type=f32)
             acc[...] = acc[...] * jnp.exp(old - top) + part
-            return peak(sc)
+            return None if dst is None else peak(sc)
 
         def pair(i, peaks):
-            peaks = half(2 * i, sa, sb, peaks)
-            return half(2 * i + 1, sb, sa, peaks)
-
-        lax.fori_loop(0, (count[k] + 1) // 2, pair, near)
+            peaks = weigh(2 * i, sa, peaks, sb)
+            return weigh(2 * i + 1, sb, peaks, sa)
+
+        blocks = meta[k, 0]
+        last = lax.fori_loop(0, blocks // 2, pair, near)
+
+        @pl.when(blocks % 2 == 1)
+        def _():
+            weigh(blocks - 1, sa, last)
+
         for c in range(0, QPK, 2):
             one, two = slice(c * ROWS, (c + 1) * ROWS), slice((c + 1) * ROWS, (c + 2) * ROWS)
             done = jnp.concatenate(
@@ -344,20 +399,13 @@
             )
             att[k, :, c * HD : (c + 2) * HD] = done.T.astype(bf16)
 
-    pltpu.make_async_copy(kv_hbm.at[pl.ds(0, GT)], pool, page_sem).wait()
-
-
-def mix(att, w, out, wv, got, acc, load, a_s, a_r):
+    pltpu.make_async_copy(kv.at[pl.ds(0, GT)], pool, page_sem).wait()
+
+
+def mix(att, w, out, got, acc, a_s, a_r):
     s, j = lax.axis_index("seq"), lax.axis_index("head")
     to = dealt(s, j)
     mine = to == s
-    loads = []
-    for r in range(8):
-        h = lax.rem(j + 8 - r, 8)
-        at = pl.multiple_of(h * QPK * HD, QPK * HD)
-        loads.append(pltpu.make_async_copy(w.at[pl.ds(at, QPK * HD)], wv.at[r], load.at[r]))
-        loads[-1].start()
-
     barrier = pltpu.get_barrier_semaphore()
     for r in range(8):
         h = lax.rem(j + r + 1, 8)
@@ -394,9 +442,10 @@
 
     for r in range(8):
         h = lax.rem(j + 8 - r, 8)
-        loads[r].wait()
         pltpu.make_async_copy(got.at[h], got.at[h], a_r.at[h]).wait()
-        part = jnp.dot(got[h], wv[r], preferred_element_type=f32)
+        part = jnp.dot(
+            got[h], w[pl.ds(pl.multiple_of(h * QPK * HD, QPK * HD), QPK * HD), :], preferred_element_type=f32
+        )
         if r == 0:
             acc[...] = part
         elif r < 7:
@@ -416,23 +465,28 @@
 DMA = pltpu.SemaphoreType.DMA
 
 
+HBM = pl.BlockSpec(memory_space=pltpu.HBM)
+
+
 def shards(hidden, w_qkv, w_out, seg_ids, live, page_table):
-    s = lax.axis_index("seq")
-    q, kv = pl.pallas_call(
+    q, kv, kx, vt, code, meta = pl.pallas_call(
         project,
         out_shape=(
             jax.ShapeDtypeStruct((STRIPES, ROWS, QPK * HD), bf16),
             jax.ShapeDtypeStruct((TOKENS, 2 * HD), bf16),
+            jax.ShapeDtypeStruct((PAD + TOKENS, 2 * HD), bf16),
+            jax.ShapeDtypeStruct((VR, PAD + TOKENS), bf16),
+            jax.ShapeDtypeStruct((TOKENS // 128, 128), jnp.int32),
+            jax.ShapeDtypeStruct((META, 128), jnp.int32),
         ),
-        in_specs=[ANY, ANY],
-        out_specs=(ANY, ANY),
+        in_specs=[VMEM, HBM, VMEM, VMEM, VMEM],
+        out_specs=(VMEM,) * 6,
         scratch_shapes=[
-            pltpu.VMEM((ROWS, D), bf16),
             pltpu.VMEM((KVH, D, 2 * HD), bf16),
             pltpu.VMEM((KVH, D, QPK * HD), bf16),
             pltpu.VMEM((KVH, ROWS, 2 * HD), bf16),
             pltpu.VMEM((KVH, ROWS, QPK * HD), bf16),
-            DMA((17,)),
+            DMA((16,)),
             DMA((7,)),
             DMA((7,)),
             DMA((8,)),
@@ -441,22 +495,9 @@
             DMA((30,)),
             DMA,
         ],
-        compiler_params=pltpu.CompilerParams(collective_id=0, has_side_effects=True, vmem_limit_bytes=40 << 20),
+        compiler_params=pltpu.CompilerParams(collective_id=0, has_side_effects=True, vmem_limit_bytes=24 << 20),
         name="project",
-    )(hidden, w_qkv)
-
-    heads = seg_ids.reshape(STRIPES, SEQ, ROWS)[:, :, 0]
-    number = jnp.arange(STRIPES, dtype=jnp.int32)
-    slots = flip(s, number % 4)
-    seg0 = jnp.sum(jnp.where(jnp.arange(SEQ, dtype=jnp.int32)[None, :] == slots[:, None], heads, 0), axis=1)
-    begin = jnp.sum((seg_ids[None, :] < seg0[:, None]).astype(jnp.int32), axis=1)
-    t0 = (16 * number + slots) * ROWS
-    count = (t0 - begin + BK - 1) // BK
-    page = s * (TOKENS // PAGE // SEQ) + jnp.arange(TOKENS // PAGE // SEQ, dtype=jnp.int32)
-    inv = jnp.sum(
-        jnp.where(page_table[None, :] == page[:, None], jnp.arange(TOKENS // PAGE, dtype=jnp.int32)[None, :], 0), axis=1
-    )
-    code = (seg_ids + 16 * (1 - live)).reshape(TOKENS // 128, 128)
+    )(hidden, w_qkv, seg_ids.reshape(-1, 128), live.reshape(-1, 128), page_table.reshape(-1, 128))
 
     att, pool = pl.pallas_call(
         attend,
@@ -464,38 +505,34 @@
             jax.ShapeDtypeStruct((STRIPES, ROWS, QPK * HD), bf16),
             jax.ShapeDtypeStruct((GT, 2 * HD), bf16),
         ),
-        in_specs=[SMEM, SMEM, SMEM, VMEM, VMEM, ANY],
-        out_specs=(VMEM, ANY),
+        in_specs=[ANY, VMEM, VMEM, VMEM, VMEM, VMEM],
+        out_specs=(VMEM, HBM),
         scratch_shapes=[
-            pltpu.VMEM((TOKENS, 2 * HD), bf16),
-            pltpu.VMEM((PAD + TOKENS, 2 * HD), bf16),
-            pltpu.VMEM((VR, PAD + TOKENS), bf16),
+            pltpu.SMEM((META, 128), jnp.int32),
             pltpu.VMEM((2 * HD, QPK * ROWS), bf16),
             pltpu.VMEM((1, QPK * ROWS), f32),
             pltpu.VMEM((VR, QPK * ROWS), f32),
             pltpu.VMEM((BK, QPK * ROWS), f32),
             pltpu.VMEM((BK, QPK * ROWS), f32),
-            DMA((STRIPES,)),
+            DMA,
             DMA,
         ],
-        compiler_params=pltpu.CompilerParams(vmem_limit_bytes=40 << 20),
+        compiler_params=pltpu.CompilerParams(vmem_limit_bytes=20 << 20),
         name="attend",
-    )(count, seg0, inv, code, q, kv)
+    )(meta, code, q, kv, kx, vt)
 
     mixed = pl.pallas_call(
         mix,
         out_shape=jax.ShapeDtypeStruct((ROWS, D), bf16),
-        in_specs=[ANY, ANY],
+        in_specs=[ANY, VMEM],
         out_specs=VMEM,
         scratch_shapes=[
-            pltpu.VMEM((KVH, QPK * HD, D), bf16),
             pltpu.VMEM((KVH, ROWS, QPK * HD), bf16),
             pltpu.VMEM((ROWS, D), f32),
             DMA((8,)),
             DMA((8,)),
-            DMA((8,)),
         ],
-        compiler_params=pltpu.CompilerParams(collective_id=1, has_side_effects=True, vmem_limit_bytes=40 << 20),
+        compiler_params=pltpu.CompilerParams(collective_id=1, has_side_effects=True, vmem_limit_bytes=12 << 20),
         name="mix",
     )(att, w_out)
     return mixed, pool.reshape(1, TOKENS // PAGE // SEQ, PAGE, 2 * HD)

time: 98.9 us -> 95.4 us (0.965)
  the two profiles are of different devices: /device:TPU:1 before, /device:TPU:109 now
where the time goes in v4:
time: 95.4 us; the launch traced here: 95.1 us
  Pallas kernels  85.7 us (90%)
  local copies, waits for them, and re-layouts  8.78 us (9%)
    pallas_call x1, Pallas kernels, shards(): pl.pallas_call(project, out_shape=(jax.ShapeDtypeStruct((STRIPES, ROWS, Q...  41.8 us
    pallas_call x1, Pallas kernels, shards(): pl.pallas_call(attend, out_shape=(jax.ShapeDtypeStruct((STRIPES, ROWS, QP...  23.4 us
    pallas_call x1, Pallas kernels, shards(): pl.pallas_call(mix, out_shape=jax.ShapeDtypeStruct((ROWS, D), bf16), in_s...  20.5 us
    unnamed x13, local copies, waits for them, and re-layouts  8.78 us

profile of v4, /device:TPU:109, one launch (start us, length us, event | category | flops | bytes accessed | tf_op | source)
XLA Modules:
  0.0 95.1 jit_solution(14654680072065252071)
XLA Ops:
  0.6 0.0 copy-start
  0.6 4.6 %copy-done = bf16[2048,3072]{1,0:T(8,128)(2,1)S(1)} copy-done((bf16[2048,3072]{1,0:T(8,128)(2,1)S(1)}, bf16[2048,3072]{1,0:T(8,128)(2,1)}, u32[]{:S(2)}) %copy-start) | copy-done | bytes 12582936
  5.2 0.0 copy-start.2
  5.2 1.0 %copy-done.2 = bf16[128,2048]{1,0:T(8,128)(2,1)S(1)} copy-done((bf16[128,2048]{1,0:T(8,128)(2,1)S(1)}, bf16[128,2048]{1,0:T(8,128)(2,1)}, u32[]{:S(2)}) %copy-start.2) | copy-done | bytes 524312
  6.2 0.0 copy-start.3
  6.3 0.8 copy-done.3
  7.1 0.0 copy-start.4
  7.1 0.8 copy-done.4
  7.9 0.0 copy-start.5
  7.9 0.7 copy-done.5
  8.6 41.8 %project.1 = (bf16[8,128,256]{2,1,0:T(8,128)(2,1)S(1)}, bf16[16384,128]{1,0:T(8,128)(2,1)S(1)}, bf16[17408,128]{1,0:T(8,128)(2,1)S(1)}, bf16[80,17408]{1,0:T(8,1...) custom-call(bf16[128,2048]{1,0:T(8,128)(2,1)S(1)} %copy-done.2, bf16[2048,3072]{1,0:T(8,128)(2,1)S(1)} %copy-done, ...), custom_call_target="tpu_custom_call" | custom-call | tf_op jit(solution)/shard_map/project/pallas_call | solution.py:472
  50.4 0.0 copy-start.1
  50.5 23.4 %attend.1 = (bf16[8,128,256]{2,1,0:T(8,128)(2,1)S(1)}, bf16[1024,128]{1,0:T(8,128)(2,1)}) custom-call(s32[72,128]{1,0:T(8,128)S(1)} %get-tuple-element.10.meta_in, s32[128,128]{1,0:T(8,128)S(1)} %get-tuple-element.11.code, bf16[8,128,256]{2,1,0:T(8,128)(2,1)S(1)} %get-tuple-element.12.q, bf16[16384,128]{1,0:T(8,128)(2,1)S(1)} %get-tuple-element.13.kv, ...), custom_call_target="tpu_custom_call" | custom-call | tf_op jit(solution)/shard_map/attend/pallas_call | solution.py:502
  73.9 0.0 copy-done.1
  73.9 20.5 %mix.1 = bf16[128,2048]{1,0:T(8,128)(2,1)S(1)} custom-call(bf16[8,128,256]{2,1,0:T(8,128)(2,1)S(1)} %get-tuple-element.16.att, bf16[2048,2048]{1,0:T(8,128)(2,1)S(1)} %copy-done.1), custom_call_target="tpu_custom_call" | custom-call | tf_op jit(solution)/shard_map/mix/pallas_call | solution.py:524
  94.3 0.8 copy.9
Async XLA Ops:
  0.6 4.6 %copy-start = (bf16[2048,3072]{1,0:T(8,128)(2,1)S(1)}, bf16[2048,3072]{1,0:T(8,128)(2,1)}, u32[]{:S(2)}) copy-start(bf16[2048,3072]{1,0:T(8,128)(2,1)} %w.2) | copy-start | bytes 37748740
  5.2 1.0 %copy-start.2 = (bf16[128,2048]{1,0:T(8,128)(2,1)S(1)}, bf16[128,2048]{1,0:T(8,128)(2,1)}, u32[]{:S(2)}) copy-start(bf16[128,2048]{1,0:T(8,128)(2,1)} %hv.1) | copy-start | bytes 1572868
  6.2 0.8 copy-start.3
  7.1 0.8 copy-start.4
  7.9 0.7 copy-start.5
  50.4 23.4 %copy-start.1 = (bf16[2048,2048]{1,0:T(8,128)(2,1)S(1)}, bf16[2048,2048]{1,0:T(8,128)(2,1)}, u32[]{:S(2)}) copy-start(bf16[2048,2048]{1,0:T(8,128)(2,1)} %w.3) | copy-start | bytes 25165828

commit v5 on v4

--- a/solution.py
+++ b/solution.py
@@ -22,40 +22,52 @@
 BK = 512
 PAD = 2 * BK
 META = STRIPES + 64
-EARLY = 3
+EARLY = 4
 NEG = -1e30
 MESH = pl.DeviceIdType.MESH
 bf16, f32 = jnp.bfloat16, jnp.float32
 
 
-MASKS = (0, 11, 13, 6)
+FLIP_Z = (1, 0, 0, 1, 1, 0, 0, 0)
+FLIP_CORE = (0, 1, 1, 0, 1, 0, 1, 0)
+FLIP_ODD = (1, 1, 1, 0, 0, 0, 0, 0)
+FLIP_EVEN = (0, 0, 1, 0, 0, 1, 1, 1)
+
+
+def bit(table, k):
+    if isinstance(k, int):
+        return table[k]
+    return sum(jnp.where(k == n, 1, 0) for n in range(8) if table[n])
 
 
 NT = (((1,), (1,)), ((), ()))
 VR = HD + 16
 
 
-def flip(value, x):
-    if isinstance(x, int):
-        bits = [(MASKS[x] >> n) % 2 for n in range(4)]
-    else:
-        low, high = x % 2, x // 2
-        both = (low + high) % 2
-        bits = [both, low, high, both]
-    return sum(((value // (1 << n) + bits[n]) % 2) * (1 << n) for n in range(4))
-
-
 def dealt(s, j):
-    return flip((s % 2) * 8 + j, (s // 2) % 4)
+    k, c, y, low = s // 2, s % 2, j // 2, j % 2
+    odd = jnp.where((y + c + bit(FLIP_ODD, k)) % 2 == 0, 1, 3)
+    even = jnp.where((y + c + bit(FLIP_EVEN, k)) % 2 == 0, 0, 2)
+    x = (k + jnp.where(y < 2, odd, even)) % 4
+    return (c + bit(FLIP_Z, k)) % 2 * 8 + x * 2 + (low + bit(FLIP_CORE, k)) % 2
+
+
+def slot_of(s, k):
+    c = (s // 8 + bit(FLIP_Z, k)) % 2
+    low = (s % 2 + bit(FLIP_CORE, k)) % 2
+    move = (s // 2 + 8 - k) % 4
+    odd = (jnp.where(move == 3, 1, 0) + c + bit(FLIP_ODD, k)) % 2
+    even = 2 + (jnp.where(move == 2, 1, 0) + c + bit(FLIP_EVEN, k)) % 2
+    return c * 8 + jnp.where(move % 2 == 1, odd, even) * 2 + low
 
 
 def held(s, k):
-    slot = flip(s, k % 4)
+    slot = slot_of(s, k)
     return 2 * k + slot // 8, slot % 8
 
 
 def project(
-    hv, w, seg, live, table, q_out, kv_out, kx, vt, code, meta,
+    hv, w, given, q_out, kv_out, kx, vt, code, meta,
     wk, wq, kvs, qs, load, a2a_s, a2a_r, q_s, q_r, g_s, g_r, loc,
 ):
     s, j = lax.axis_index("seq"), lax.axis_index("head")
@@ -73,6 +85,7 @@
         g = lax.rem(j + r + 1, 8)
         col = pl.multiple_of(g * COLS, 128)
         loads.append(pltpu.make_async_copy(w.at[:, pl.ds(col, QPK * HD)], wq.at[r], load.at[8 + r]))
+        loads[-1].start()
 
     def block(zz, xx, cc):
         return zz * 8 + xx * 2 + cc
@@ -95,24 +108,24 @@
 
     down = lax.broadcasted_iota(jnp.int32, (128, 128), 0)
     along = lax.broadcasted_iota(jnp.int32, (128, 128), 1)
-    eye = (down == along).astype(bf16)
     pick = (along[:HD] == down[:HD] + HD).astype(bf16)
     marks = (down >= HD) & (down < HD + SEGS)
     mark_row = (along[:1] >= HD) & (along[:1] < HD + SEGS)
 
     def tables():
-        code[...] = seg[...] + 16 * (1 - live[...])
+        code[...] = given[: TOKENS // 128]
+        seg = code[...] & 15
         lane = along[:1]
         for k in range(STRIPES):
-            stripe = 16 * k + flip(s, k % 4)
-            own = seg[pl.ds(stripe, 1), :][:, :1]
-            before = jnp.where(seg[...] < own, 1.0, 0.0)
+            stripe = 16 * k + slot_of(s, k)
+            own = code[pl.ds(stripe, 1), :][:, :1] & 15
+            before = jnp.where(seg < own, 1.0, 0.0)
             begin = jnp.sum(jnp.sum(before, axis=0, keepdims=True), axis=1, keepdims=True).astype(jnp.int32)
             blocks = lax.shift_right_logical(stripe * ROWS - begin + BK - 1, BK.bit_length() - 1)
             meta[k : k + 1, :] = jnp.where(lane == 0, blocks, own)
         at = jnp.zeros((64, 128), f32)
         for n in range(TOKENS // PAGE // 128):
-            hit = table[n : n + 1, :] == 64 * s + down[:64]
+            hit = given[TOKENS // 128 + n : TOKENS // 128 + n + 1, :] == 64 * s + down[:64]
             at += jnp.where(hit, (n * 128 + along[:64]).astype(f32), 0.0)
         logical = jnp.sum(at, axis=1, keepdims=True).astype(jnp.int32)
         meta[STRIPES:, :] = jnp.broadcast_to(logical, (64, 128))
@@ -120,44 +133,41 @@
         vt[:HD, :PAD] = jnp.zeros((HD, PAD), bf16)
         vt[HD:, :] = jnp.ones((VR - HD, PAD + TOKENS), bf16)
 
-    def mark_keys(first, stop):
-        @pl.loop(first, stop)
-        def _(i):
-            for n in range(8):
-                row = code[pl.ds(i * 8 + n, 1), :]
-                mark = jnp.where(marks & (row != down - HD), NEG, 0.0).astype(bf16)
-                mark = lax.dot_general(eye, mark, NT, preferred_element_type=f32).astype(bf16)
-                kx[pl.ds(pl.multiple_of(PAD + (i * 8 + n) * 128, 128), 128), :] = mark
-
     def use(b, h):
         at = pl.multiple_of(b * GT + h * (GT // 2), 128)
         to = pl.multiple_of(PAD + at, 128)
         rows = kv_out[pl.ds(at, GT // 2), :]
         vt[:HD, pl.ds(to, GT // 2)] = lax.dot_general(pick, rows, NT, preferred_element_type=f32).astype(bf16)
-        kx[pl.ds(to, GT // 2), :] = jnp.where(along[:1] < HD, rows, kx[pl.ds(to, GT // 2), :])
-
-    row0 = pl.multiple_of(s * GT + j * ROWS, ROWS)
-    sends = []
+        for n in range(GT // 2 // 128):
+            row = given[pl.ds(b * (GT // 128) + h * (GT // 256) + n, 1), :]
+            mark = jnp.where(marks & (row != down - HD), NEG, 0.0).T.astype(bf16)
+            kx[pl.ds(to + n * 128, 128), :] = jnp.where(along[:1] < HD, rows[n * 128 : (n + 1) * 128], mark)
+
+    def query(r):
+        loads[8 + r].wait()
+        qs[r] = (jnp.dot(hv[...], wq[r], preferred_element_type=f32).astype(bf16) * 0.015625).astype(bf16)
+
     for r in range(8):
-        g = lax.rem(j + r + 1, 8)
         loads[r].wait()
         kvs[r] = jnp.dot(hv[...], wk[r], preferred_element_type=f32).astype(bf16)
-        if r == 0:
-            pl.semaphore_wait(barrier, jnp.where(mine, 18, 19))
-        if r < 7:
-            cp = pltpu.make_async_remote_copy(
-                src_ref=kvs.at[r],
-                dst_ref=kv_out.at[pl.ds(row0, ROWS)],
-                send_sem=a2a_s.at[r],
-                recv_sem=a2a_r.at[r],
-                device_id=(s, g),
-                device_id_type=MESH,
-            )
-            cp.start()
-            sends.append(cp)
-        else:
-            own_kv = pltpu.make_async_copy(kvs.at[r], kv_out.at[pl.ds(row0, ROWS)], loc)
-            own_kv.start()
+    for r in range(EARLY):
+        query(r)
+    row0 = pl.multiple_of(s * GT + j * ROWS, ROWS)
+    own_kv = pltpu.make_async_copy(kvs.at[7], kv_out.at[pl.ds(row0, ROWS)], loc)
+    own_kv.start()
+    pl.semaphore_wait(barrier, jnp.where(mine, 18, 19))
+    sends = []
+    for r in range(7):
+        cp = pltpu.make_async_remote_copy(
+            src_ref=kvs.at[r],
+            dst_ref=kv_out.at[pl.ds(row0, ROWS)],
+            send_sem=a2a_s.at[r],
+            recv_sem=a2a_r.at[r],
+            device_id=(s, lax.rem(j + r + 1, 8)),
+            device_id_type=MESH,
+        )
+        cp.start()
+        sends.append(cp)
 
     H = GT // 2
     R, L, Z, C = range(4)
@@ -188,10 +198,6 @@
     slot = s // 2
     qsends = []
 
-    def query(r):
-        loads[8 + r].wait()
-        qs[r] = (jnp.dot(hv[...], wq[r], preferred_element_type=f32).astype(bf16) * 0.015625).astype(bf16)
-
     def send_query(r):
         cp = pltpu.make_async_remote_copy(
             src_ref=qs.at[r],
@@ -215,11 +221,10 @@
                 pltpu.make_async_copy(qs.at[7], q_out.at[slot], q_r.at[slot]).start()
 
     for r in range(8):
-        loads[8 + r].start()
+        if r >= EARLY:
+            query(r)
+        send_query(r)
     tables()
-    mark_keys(0, 8)
-    for r in range(EARLY):
-        query(r)
     own_kv.wait()
     for r in range(7):
         source = lax.rem(j + 7 - r, 8)
@@ -233,11 +238,6 @@
     pass_on(me, 1, R)
     pass_on(me, 0, L, C)
     pass_on(me, 1, C)
-    for r in range(EARLY, 8):
-        query(r)
-    for r in range(8):
-        send_query(r)
-    mark_keys(8, 16)
     d = 1 - c
     ome, ol, or_, of = block(zh, x, d), block(zh, left, d), block(zh, right, d), block(zh, far, d)
     oz, ozl, ozr, ozf = block(1 - zh, x, d), block(1 - zh, left, d), block(1 - zh, right, d), block(1 - zh, far, d)
@@ -341,7 +341,7 @@
 
     @pl.loop(0, STRIPES)
     def _(k):
-        stripe = 16 * k + flip(s, k % 4)
+        stripe = 16 * k + slot_of(s, k)
         own = meta[k, 1]
         here = pl.multiple_of(PAD + stripe * ROWS, 128)
         for c in range(0, QPK, 2):
@@ -468,8 +468,8 @@
 HBM = pl.BlockSpec(memory_space=pltpu.HBM)
 
 
-def shards(hidden, w_qkv, w_out, seg_ids, live, page_table):
-    q, kv, kx, vt, code, meta = pl.pallas_call(
+def projected(hidden, w_qkv, given):
+    return pl.pallas_call(
         project,
         out_shape=(
             jax.ShapeDtypeStruct((STRIPES, ROWS, QPK * HD), bf16),
@@ -479,7 +479,7 @@
             jax.ShapeDtypeStruct((TOKENS // 128, 128), jnp.int32),
             jax.ShapeDtypeStruct((META, 128), jnp.int32),
         ),
-        in_specs=[VMEM, HBM, VMEM, VMEM, VMEM],
+        in_specs=[VMEM, HBM, VMEM],
         out_specs=(VMEM,) * 6,
         scratch_shapes=[
             pltpu.VMEM((KVH, D, 2 * HD), bf16),
@@ -495,10 +495,14 @@
             DMA((30,)),
             DMA,
         ],
-        compiler_params=pltpu.CompilerParams(collective_id=0, has_side_effects=True, vmem_limit_bytes=24 << 20),
+        compiler_params=pltpu.CompilerParams(collective_id=0, has_side_effects=True, vmem_limit_bytes=34 << 20),
         name="project",
-    )(hidden, w_qkv, seg_ids.reshape(-1, 128), live.reshape(-1, 128), page_table.reshape(-1, 128))
-
+    )(hidden, w_qkv, given)
+
+
+def shards(hidden, w_qkv, w_out, seg_ids, live, page_table):
+    given = jnp.concatenate([seg_ids + 16 * (1 - live), page_table]).reshape(-1, 128)
+    q, kv, kx, vt, code, meta = projected(hidden, w_qkv, given)
     att, pool = pl.pallas_call(
         attend,
         out_shape=(

time: 95.4 us -> 84.8 us (0.89)
  the two profiles are of different devices: /device:TPU:109 before, /device:TPU:0 now
where the time goes in v5:
time: 84.8 us; the launch traced here: 84.7 us
  Pallas kernels  80.2 us (95%)
  other arithmetic  1.99 us (2%)
  local copies, waits for them, and re-layouts  1.85 us (2%)
    pallas_call x1, Pallas kernels, projected(): pl.pallas_call(project, out_shape=(jax.ShapeDtypeStruct((STRIPES, ROWS, Q...  41.1 us
    pallas_call x1, Pallas kernels, shards(): pl.pallas_call(attend, out_shape=(jax.ShapeDtypeStruct((STRIPES, ROWS, QP...  23.7 us
    pallas_call x1, Pallas kernels, shards(): pl.pallas_call(mix, out_shape=jax.ShapeDtypeStruct((ROWS, D), bf16), in_s...  15.4 us
    unnamed x7, local copies, waits for them, and re-layouts  1.85 us

profile of v5, /device:TPU:0, one launch (start us, length us, event | category | flops | bytes accessed | tf_op | source)
XLA Modules:
  0.0 84.7 jit_solution(17159382755839415819)
XLA Ops:
  0.6 0.0 slice-start
  0.6 1.0 %multiply_add_fusion = s32[16384]{0:T(1024)S(1)} fusion(s32[16384]{0:T(1024)} %param.9, s32[16384]{0:T(1024)} %param.10), kind=kLoop, calls=%fused_computation.1 | loop fusion | flops 49152 | bytes 196608 | tf_op jit(solution)/shard_map/add | solution.py:504
  1.7 1.0 %add_bitcast_fusion.given = s32[136,128]{1,0:T(8,128)S(1)} fusion(s32[1024]{0:T(1024)} %param.11, s32[16384]{0:T(1024)S(1)} %multiply_add_fusion), kind=kLoop, calls=%fused_computation | loop fusion | flops 17408 | bytes 139264 | tf_op jit(solution)/shard_map/reshape | solution.py:504
  2.6 0.0 copy-start
  2.6 1.0 %copy-done = bf16[128,2048]{1,0:T(8,128)(2,1)S(1)} copy-done((bf16[128,2048]{1,0:T(8,128)(2,1)S(1)}, bf16[128,2048]{1,0:T(8,128)(2,1)}, u32[]{:S(2)}) %copy-start) | copy-done | bytes 524312
  3.7 0.0 slice-start.1
  3.7 41.1 %project.1 = (bf16[8,128,256]{2,1,0:T(8,128)(2,1)S(1)}, bf16[16384,128]{1,0:T(8,128)(2,1)S(1)}, bf16[17408,128]{1,0:T(8,128)(2,1)S(1)}, bf16[80,17408]{1,0:T(8,1...) custom-call(bf16[128,2048]{1,0:T(8,128)(2,1)S(1)} %copy-done, bf16[2048,3072]{1,0:T(8,128)(2,1)} %w.2, ...), custom_call_target="tpu_custom_call" | custom-call | tf_op jit(solution)/shard_map/project/pallas_call | solution.py:472
  44.8 23.7 %attend.1 = (bf16[8,128,256]{2,1,0:T(8,128)(2,1)S(1)}, bf16[1024,128]{1,0:T(8,128)(2,1)}) custom-call(s32[72,128]{1,0:T(8,128)S(1)} %get-tuple-element.10.meta_in, s32[128,128]{1,0:T(8,128)S(1)} %get-tuple-element.11.code, bf16[8,128,256]{2,1,0:T(8,128)(2,1)S(1)} %get-tuple-element.12.q, bf16[16384,128]{1,0:T(8,128)(2,1)S(1)} %get-tuple-element.13.kv, ...), custom_call_target="tpu_custom_call" | custom-call | tf_op jit(solution)/shard_map/attend/pallas_call | solution.py:506
  68.5 0.0 slice-done
  68.5 0.0 slice-done.1
  68.6 15.4 %mix.1 = bf16[128,2048]{1,0:T(8,128)(2,1)S(1)} custom-call(bf16[8,128,256]{2,1,0:T(8,128)(2,1)S(1)} %get-tuple-element.16.att, bf16[2048,2048]{1,0:T(8,128)(2,1)S(1)} %bitcast.4), custom_call_target="tpu_custom_call" | custom-call | tf_op jit(solution)/shard_map/mix/pallas_call | solution.py:528
  83.9 0.8 copy.9
  (1 shorter events, 0.0 us)
Async XLA Ops:
  0.6 67.9 %slice-start = ((s8[8388608]{0:T(1024)(128)(4,1)}), s8[4194304]{0:T(1024)(128)(4,1)S(1)}, s32[]{:S(2)}) async-start(s8[8388608]{0:T(1024)(128)(4,1)} %bitcast.3), calls=%async_computation | async-start | bytes 8388608
  2.6 1.0 %copy-start = (bf16[128,2048]{1,0:T(8,128)(2,1)S(1)}, bf16[128,2048]{1,0:T(8,128)(2,1)}, u32[]{:S(2)}) copy-start(bf16[128,2048]{1,0:T(8,128)(2,1)} %hv.1) | copy-start | bytes 1572868
  3.7 64.9 %slice-start.1 = ((s8[8388608]{0:T(1024)(128)(4,1)}), s8[4194304]{0:T(1024)(128)(4,1)S(1)}, s32[]{:S(2)}) async-start(s8[8388608]{0:T(1024)(128)(4,1)} %bitcast.3), calls=%async_computation.1 | async-start | bytes 8388608

commit v6 on v5

--- a/solution.py
+++ b/solution.py
@@ -21,7 +21,10 @@
 STRIPES = 8
 BK = 512
 PAD = 2 * BK
+ITEMS = STRIPES * (TOKENS // BK) + 8
 META = STRIPES + 64
+CHUNKS = 2
+CH = GT // CHUNKS
 EARLY = 4
 NEG = -1e30
 MESH = pl.DeviceIdType.MESH
@@ -113,7 +116,7 @@
     mark_row = (along[:1] >= HD) & (along[:1] < HD + SEGS)
 
     def tables():
-        code[...] = given[: TOKENS // 128]
+        code[...] = given[...] & 31
         seg = code[...] & 15
         lane = along[:1]
         for k in range(STRIPES):
@@ -125,7 +128,7 @@
             meta[k : k + 1, :] = jnp.where(lane == 0, blocks, own)
         at = jnp.zeros((64, 128), f32)
         for n in range(TOKENS // PAGE // 128):
-            hit = given[TOKENS // 128 + n : TOKENS // 128 + n + 1, :] == 64 * s + down[:64]
+            hit = lax.shift_right_logical(given[n : n + 1, :], 5) == 64 * s + down[:64]
             at += jnp.where(hit, (n * 128 + along[:64]).astype(f32), 0.0)
         logical = jnp.sum(at, axis=1, keepdims=True).astype(jnp.int32)
         meta[STRIPES:, :] = jnp.broadcast_to(logical, (64, 128))
@@ -134,12 +137,12 @@
         vt[HD:, :] = jnp.ones((VR - HD, PAD + TOKENS), bf16)
 
     def use(b, h):
-        at = pl.multiple_of(b * GT + h * (GT // 2), 128)
+        at = pl.multiple_of(b * GT + h * CH, 128)
         to = pl.multiple_of(PAD + at, 128)
-        rows = kv_out[pl.ds(at, GT // 2), :]
-        vt[:HD, pl.ds(to, GT // 2)] = lax.dot_general(pick, rows, NT, preferred_element_type=f32).astype(bf16)
-        for n in range(GT // 2 // 128):
-            row = given[pl.ds(b * (GT // 128) + h * (GT // 256) + n, 1), :]
+        rows = kv_out[pl.ds(at, CH), :]
+        vt[:HD, pl.ds(to, CH)] = lax.dot_general(pick, rows, NT, preferred_element_type=f32).astype(bf16)
+        for n in range(CH // 128):
+            row = code[pl.ds(b * (GT // 128) + h * (CH // 128) + n, 1), :]
             mark = jnp.where(marks & (row != down - HD), NEG, 0.0).T.astype(bf16)
             kx[pl.ds(to + n * 128, 128), :] = jnp.where(along[:1] < HD, rows[n * 128 : (n + 1) * 128], mark)
 
@@ -169,18 +172,18 @@
         cp.start()
         sends.append(cp)
 
-    H = GT // 2
     R, L, Z, C = range(4)
+    held_at = {}
 
     def half(b, h):
-        return kv_out.at[pl.ds(pl.multiple_of(b * GT + h * H, 128), H)]
-
-    count = [0]
+        return kv_out.at[pl.ds(pl.multiple_of(held_at[b] * GT + h * CH, 128), CH)]
+
+    copies = {}
 
     def pass_on(b, h, *to_peers):
         for peer in to_peers:
-            i = count[0]
-            count[0] += 1
+            i = len(copies)
+            copies[b, h, peer] = i
             cp = pltpu.make_async_remote_copy(
                 src_ref=half(b, h),
                 dst_ref=half(b, h),
@@ -192,8 +195,8 @@
             cp.start()
             sends.append(cp)
 
-    def arrived(b, h, i):
-        pltpu.make_async_copy(half(b, h), half(b, h), g_r.at[i]).wait()
+    def arrived(b, h, sent, peer):
+        pltpu.make_async_copy(half(b, h), half(b, h), g_r.at[copies[sent, h, peer]]).wait()
 
     slot = s // 2
     qsends = []
@@ -230,82 +233,89 @@
         source = lax.rem(j + 7 - r, 8)
         there = kv_out.at[pl.ds(pl.multiple_of(s * GT + source * ROWS, ROWS), ROWS)]
         pltpu.make_async_copy(there, there, a2a_r.at[r]).wait()
-    me = block(zh, x, c)
-    bl, br, bf = block(zh, left, c), block(zh, right, c), block(zh, far, c)
-    zm, zl, zr, zf = block(1 - zh, x, c), block(1 - zh, left, c), block(1 - zh, right, c), block(1 - zh, far, c)
-    pass_on(me, 0, R, Z)
-    pass_on(me, 1, L, Z)
-    pass_on(me, 1, R)
-    pass_on(me, 0, L, C)
-    pass_on(me, 1, C)
-    d = 1 - c
-    ome, ol, or_, of = block(zh, x, d), block(zh, left, d), block(zh, right, d), block(zh, far, d)
-    oz, ozl, ozr, ozf = block(1 - zh, x, d), block(1 - zh, left, d), block(1 - zh, right, d), block(1 - zh, far, d)
-    arrived(bl, 0, 0)
-    pass_on(bl, 0, R, C)
-    arrived(br, 1, 2)
-    pass_on(br, 1, L, C)
-    arrived(zm, 0, 1)
-    pass_on(zm, 0, R, L, C)
-    use(me, 0)
-    use(me, 1)
-    arrived(zm, 1, 3)
-    pass_on(zm, 1, R, L, C)
-    arrived(bl, 1, 4)
-    pass_on(bl, 1, C)
-    arrived(br, 0, 5)
-    pass_on(br, 0, C)
-    use(bl, 0)
-    use(br, 1)
-    arrived(bf, 0, 8)
-    pass_on(bf, 0, Z, C)
-    arrived(bf, 1, 10)
-    pass_on(bf, 1, Z, C)
-
-    def other(b, h, i):
-        arrived(b, h, i)
-        use(b, h)
-
-    use(zm, 0)
-    use(zm, 1)
-    use(bl, 1)
-    use(br, 0)
-    other(ome, 0, 6)
-    other(ome, 1, 7)
-    other(ol, 0, 9)
-    other(or_, 1, 11)
-    other(oz, 0, 14)
-    arrived(zl, 0, 12)
-    pass_on(zl, 0, C)
-    arrived(zr, 0, 13)
-    pass_on(zr, 0, C)
-    other(oz, 1, 17)
-    other(ol, 1, 18)
-    other(or_, 0, 19)
-    use(bf, 0)
-    use(bf, 1)
-    other(of, 0, 21)
-    other(of, 1, 23)
-    arrived(zf, 0, 20)
-    pass_on(zf, 0, C)
-    use(zl, 0)
-    use(zr, 0)
-    arrived(zl, 1, 15)
-    pass_on(zl, 1, C)
-    arrived(zr, 1, 16)
-    pass_on(zr, 1, C)
-    arrived(zf, 1, 22)
-    pass_on(zf, 1, C)
-    use(zf, 0)
-    other(ozl, 0, 24)
-    other(ozr, 0, 25)
-    use(zl, 1)
-    use(zr, 1)
-    other(ozf, 0, 26)
-    use(zf, 1)
-    other(ozl, 1, 27)
-    other(ozr, 1, 28)
-    other(ozf, 1, 29)
+    places = (("m", x), ("l", left), ("r", right), ("f", far))
+    for half_z, zz in (("o", zh), ("z", 1 - zh)):
+        for core, cc in (("", c), ("c", 1 - c)):
+            for name, xx in places:
+                held_at[half_z + name + core] = block(zz, xx, cc)
+    low, high = range(CHUNKS // 2), range(CHUNKS // 2, CHUNKS)
+    for h in low:
+        pass_on("om", h, R, Z)
+    for h in high:
+        pass_on("om", h, L, Z)
+    for h in high:
+        pass_on("om", h, R)
+    for h in low:
+        pass_on("om", h, L, C)
+    for h in high:
+        pass_on("om", h, C)
+
+    def ready(b, *chunks):
+        for h in chunks:
+            use(held_at[b], h)
+
+    def other(b, *chunks):
+        for h in chunks:
+            arrived(b + "c", h, b, C)
+            use(held_at[b + "c"], h)
+
+    for h, g in zip(low, high, strict=True):
+        arrived("ol", h, "om", R)
+        pass_on("ol", h, R, C)
+        arrived("or", g, "om", L)
+        pass_on("or", g, L, C)
+        ready("om", h)
+    for h in (*low, *high):
+        arrived("zm", h, "om", Z)
+        pass_on("zm", h, R, L, C)
+        if h in high:
+            ready("om", h)
+    for h, g in zip(low, high, strict=True):
+        arrived("ol", g, "om", R)
+        pass_on("ol", g, C)
+        arrived("or", h, "om", L)
+        pass_on("or", h, C)
+        ready("ol", h)
+        ready("or", g)
+    for h, g in zip(low, high, strict=True):
+        arrived("of", h, "ol", R)
+        pass_on("of", h, Z, C)
+        arrived("of", g, "or", L)
+        pass_on("of", g, Z, C)
+        ready("zm", h, g)
+        other("om", h, g)
+    ready("ol", *high)
+    ready("or", *low)
+    other("ol", *low)
+    other("or", *high)
+    other("zm", *low)
+    for h in (*low, *high):
+        arrived("zl", h, "zm", R)
+        pass_on("zl", h, C)
+        arrived("zr", h, "zm", L)
+        pass_on("zr", h, C)
+        if h in low:
+            other("zm", h + CHUNKS // 2)
+            other("ol", h + CHUNKS // 2)
+            other("or", h)
+        else:
+            ready("of", h - CHUNKS // 2, h)
+            other("of", h - CHUNKS // 2, h)
+            ready("zl", h - CHUNKS // 2)
+            ready("zr", h - CHUNKS // 2)
+    for h, g in zip(low, high, strict=True):
+        arrived("zf", h, "of", Z)
+        pass_on("zf", h, C)
+        ready("zl", g)
+        arrived("zf", g, "of", Z)
+        pass_on("zf", g, C)
+        ready("zr", g)
+        other("zl", h)
+        other("zr", h)
+    ready("zf", *low, *high)
+    other("zl", *high)
+    other("zr", *high)
+    other("zf", *low, *high)
 
     for k in range(STRIPES):
         pltpu.make_async_copy(q_out.at[k], q_out.at[k], q_r.at[k]).wait()
@@ -317,87 +327,104 @@
         qsends[7].wait_send()
 
 
-def attend(meta_in, code, q, kv, kx, vt, att, pool, meta, qt, m, acc, sa, sb, sem, page_sem):
+BATCH = 8
+
+
+def attend(meta_in, code, q, kv, kx, vt, att, pool, meta, item_k, item_at, qt, m, acc, sa, sb, sem, page_sem):
     s = lax.axis_index("seq")
     fetch = pltpu.make_async_copy(meta_in, meta, sem)
     fetch.start()
     down = lax.broadcasted_iota(jnp.int32, (128, 128), 0)
     along = lax.broadcasted_iota(jnp.int32, (128, 128), 1)
+    wide = QPK * ROWS
+    fetch.wait()
+
+    def place(k):
+        return pl.multiple_of(PAD + (16 * k + slot_of(s, k)) * ROWS, 128)
+
+    def stripe_items(k, n):
+        here = place(k)
+
+        def one(b, n):
+            item_k[n] = k
+            item_at[n] = here - (b + 1) * BK
+            return n + 1
+
+        return lax.fori_loop(0, meta[k, 0], one, n)
+
+    total = lax.fori_loop(0, STRIPES, stripe_items, 0)
+    for n in range(3):
+        item_k[total + n] = STRIPES - 1
+        item_at[total + n] = 0
 
     def peak(sc):
         return jnp.max(sc.reshape(sc.shape[0] // 8, 8, sc.shape[1]), axis=0)
 
-    def scores(first):
-        keys = kx[pl.ds(pl.multiple_of(first, 128), BK), :]
-        return jnp.dot(keys, qt[...], preferred_element_type=f32)
-
-    fetch.wait()
-
-    @pl.loop(0, TOKENS // PAGE // SEQ)
-    def _(i):
-        at = pl.multiple_of(meta[STRIPES + i, 0] * PAGE, PAGE)
-        to = pl.multiple_of(i * PAGE, PAGE)
-        pltpu.make_async_copy(kv.at[pl.ds(at, PAGE)], pool.at[pl.ds(to, PAGE)], page_sem).start()
-
-    @pl.loop(0, STRIPES)
-    def _(k):
-        stripe = 16 * k + slot_of(s, k)
-        own = meta[k, 1]
-        here = pl.multiple_of(PAD + stripe * ROWS, 128)
-        for c in range(0, QPK, 2):
-            t = q[k, :, c * HD : (c + 2) * HD].T
-            qt[:HD, c * ROWS : (c + 1) * ROWS] = t[:HD]
-            qt[:HD, (c + 1) * ROWS : (c + 2) * ROWS] = t[HD:]
-        qt[HD:, :] = (lax.broadcasted_iota(jnp.int32, (HD, QPK * ROWS), 0) == own).astype(bf16)
-
-        sc = scores(here - BK)
-        sa[...] = sc
-        near = peak(sc)
-
-        row = code[pl.ds(stripe, 1), :]
-        ct = jnp.broadcast_to(row, (ROWS, ROWS))
-        cu = ct.T
-        allowed = ((cu & 15) == (ct & 15)) & (down <= along) & ((cu < 16) | (down == along))
-        same = (row & 15) == own
-        sc = jnp.dot(kx[pl.ds(here, ROWS), :HD], qt[:HD, :], preferred_element_type=f32)
-        sc = jnp.concatenate(
-            [jnp.where(allowed, sc[:, c * ROWS : (c + 1) * ROWS], NEG) for c in range(QPK)], axis=1
-        )
+    @pl.loop(0, STRIPES // BATCH)
+    def _(group):
+        for n in range(64 * BATCH // STRIPES):
+            i = group * (64 * BATCH // STRIPES) + n
+            at = pl.multiple_of(meta[STRIPES + i, 0] * PAGE, PAGE)
+            to = pl.multiple_of(i * PAGE, PAGE)
+            pltpu.make_async_copy(kv.at[pl.ds(at, PAGE)], pool.at[pl.ds(to, PAGE)], page_sem).start()
+        parts, same = [], []
+        for n in range(BATCH):
+            k = group * BATCH + n
+            own = meta[k, 1]
+            here = place(k)
+            tq = [q[k, :, c * HD : (c + 2) * HD].T for c in range(0, QPK, 2)]
+            tq = jnp.concatenate([h for t in tq for h in (t[:HD], t[HD:])], axis=1)
+            qt[k, :HD, :] = tq
+            qt[k, HD:, :] = (lax.broadcasted_iota(jnp.int32, (HD, wide), 0) == own).astype(bf16)
+            row = code[pl.ds((here - PAD) // 128, 1), :]
+            ct = jnp.broadcast_to(row, (ROWS, ROWS))
+            cu = ct.T
+            allowed = ((cu & 15) == (ct & 15)) & (down <= along) & ((cu < 16) | (down == along))
+            sc = jnp.dot(kx[pl.ds(here, ROWS), :HD], tq, preferred_element_type=f32)
+            parts += [jnp.where(allowed, sc[:, c * ROWS : (c + 1) * ROWS], NEG) for c in range(QPK)]
+            same += [(row & 15) == own] * QPK
+        sc = jnp.concatenate(parts, axis=1)
         top = jnp.max(peak(sc), axis=0, keepdims=True)
         p = jnp.exp(sc - top).astype(bf16)
-        acc[...] = jnp.dot(vt[:, pl.ds(here, ROWS)], p, preferred_element_type=f32)
-        m[...] = jnp.where(jnp.concatenate([same] * QPK, axis=1), top, -NEG)
-
-        def weigh(b, src, peaks, dst=None):
-            first = here - (b + 1) * BK
-            old = m[...]
-            top = jnp.maximum(old, jnp.max(peaks, axis=0, keepdims=True))
-            m[...] = top
-            if dst is not None:
-                sc = scores(first - BK)
-                dst[...] = sc
-            p = jnp.exp(src[...] - top).astype(bf16)
-            part = jnp.dot(vt[:, pl.ds(pl.multiple_of(first, 128), BK)], p, preferred_element_type=f32)
-            acc[...] = acc[...] * jnp.exp(old - top) + part
-            return None if dst is None else peak(sc)
-
-        def pair(i, peaks):
-            peaks = weigh(2 * i, sa, peaks, sb)
-            return weigh(2 * i + 1, sb, peaks, sa)
-
-        blocks = meta[k, 0]
-        last = lax.fori_loop(0, blocks // 2, pair, near)
-
-        @pl.when(blocks % 2 == 1)
-        def _():
-            weigh(blocks - 1, sa, last)
-
-        for c in range(0, QPK, 2):
-            one, two = slice(c * ROWS, (c + 1) * ROWS), slice((c + 1) * ROWS, (c + 2) * ROWS)
-            done = jnp.concatenate(
-                [acc[:HD, one] / acc[HD : HD + 1, one], acc[:HD, two] / acc[HD : HD + 1, two]], axis=0
-            )
-            att[k, :, c * HD : (c + 2) * HD] = done.T.astype(bf16)
+        start = jnp.where(jnp.concatenate(same, axis=1), top, -NEG)
+        for n in range(BATCH):
+            k = group * BATCH + n
+            cols = slice(n * wide, (n + 1) * wide)
+            acc[k] = jnp.dot(vt[:, pl.ds(place(k), ROWS)], p[:, cols], preferred_element_type=f32)
+            m[k] = start[:, cols]
+
+    def scores(n):
+        keys = kx[pl.ds(pl.multiple_of(item_at[n], 128), BK), :]
+        return jnp.dot(keys, qt[item_k[n]], preferred_element_type=f32)
+
+    def weigh(n, src, dst, peaks):
+        k = item_k[n]
+        old = m[k]
+        top = jnp.maximum(old, jnp.max(peaks, axis=0, keepdims=True))
+        m[k] = top
+        sc = scores(n + 1)
+        dst[...] = sc
+        p = jnp.exp(src[...] - top).astype(bf16)
+        part = jnp.dot(vt[:, pl.ds(pl.multiple_of(item_at[n], 128), BK)], p, preferred_element_type=f32)
+        acc[k] = acc[k] * jnp.exp(old - top) + part
+        return peak(sc)
+
+    def pair(i, peaks):
+        peaks = weigh(2 * i, sa, sb, peaks)
+        return weigh(2 * i + 1, sb, sa, peaks)
+
+    sc = scores(0)
+    sa[...] = sc
+    lax.fori_loop(0, (total + 1) // 2, pair, peak(sc))
+
+    @pl.loop(0, STRIPES // BATCH)
+    def _(group):
+        for n in range(BATCH):
+            k = group * BATCH + n
+            done = acc[k, :HD, :] / acc[k, HD : HD + 1, :]
+            for c in range(0, QPK, 2):
+                two = [done[:, (c + d) * ROWS : (c + d + 1) * ROWS] for d in range(2)]
+                att[k, :, c * HD : (c + 2) * HD] = jnp.concatenate(two, axis=0).T.astype(bf16)
 
     pltpu.make_async_copy(kv.at[pl.ds(0, GT)], pool, page_sem).wait()
 
@@ -491,8 +518,8 @@
             DMA((7,)),
             DMA((8,)),
             DMA((8,)),
-            DMA((30,)),
-            DMA((30,)),
+            DMA((15 * CHUNKS,)),
+            DMA((15 * CHUNKS,)),
             DMA,
         ],
         compiler_params=pltpu.CompilerParams(collective_id=0, has_side_effects=True, vmem_limit_bytes=34 << 20),
@@ -501,7 +528,8 @@
 
 
 def shards(hidden, w_qkv, w_out, seg_ids, live, page_table):
-    given = jnp.concatenate([seg_ids + 16 * (1 - live), page_table]).reshape(-1, 128)
+    pages = jnp.pad(page_table, (0, TOKENS - TOKENS // PAGE))
+    given = (seg_ids + 16 * (1 - live) + 32 * pages).reshape(-1, 128)
     q, kv, kx, vt, code, meta = projected(hidden, w_qkv, given)
     att, pool = pl.pallas_call(
         attend,
@@ -513,9 +541,11 @@
         out_specs=(VMEM, HBM),
         scratch_shapes=[
             pltpu.SMEM((META, 128), jnp.int32),
-            pltpu.VMEM((2 * HD, QPK * ROWS), bf16),
-            pltpu.VMEM((1, QPK * ROWS), f32),
-            pltpu.VMEM((VR, QPK * ROWS), f32),
+            pltpu.SMEM((ITEMS,), jnp.int32),
+            pltpu.SMEM((ITEMS,), jnp.int32),
+            pltpu.VMEM((STRIPES, 2 * HD, QPK * ROWS), bf16),
+            pltpu.VMEM((STRIPES, 1, QPK * ROWS), f32),
+            pltpu.VMEM((STRIPES, VR, QPK * ROWS), f32),
             pltpu.VMEM((BK, QPK * ROWS), f32),
             pltpu.VMEM((BK, QPK * ROWS), f32),
             DMA,

time: 84.8 us -> 79.7 us (0.940); the launches traced: 84.7 us -> 78.4 us
  Pallas kernels: 80.2 us -> 75 us
  other arithmetic: 1.99 us -> 0.9 us
    pallas_call x1, Pallas kernels: 23.7 us -> 15.2 us  [shards(): pl.pallas_call(attend, out_shape=(jax.ShapeDtypeStruct((STRIPES, ROWS, QP...]
    pallas_call x1, Pallas kernels: 15.4 us -> 18.9 us  [shards(): pl.pallas_call(mix, out_shape=jax.ShapeDtypeStruct((ROWS, D), bf16), in_s...]
    add x1 -> x0, other arithmetic: 1.03 us -> none  [shards(): seg_ids + 16 * (1 - live)]
    unnamed x7 -> x5, local copies, waits for them, and re-layouts: 1.85 us -> 1.84 us
where the time goes in v6:
time: 79.7 us; the launch traced here: 78.4 us
  Pallas kernels  75 us (94%)
  local copies, waits for them, and re-layouts  1.84 us (2%)
  other arithmetic  0.9 us (1%)
    pallas_call x1, Pallas kernels, projected(): pl.pallas_call(project, out_shape=(jax.ShapeDtypeStruct((STRIPES, ROWS, Q...  40.9 us
    pallas_call x1, Pallas kernels, shards(): pl.pallas_call(mix, out_shape=jax.ShapeDtypeStruct((ROWS, D), bf16), in_s...  18.9 us
    pallas_call x1, Pallas kernels, shards(): pl.pallas_call(attend, out_shape=(jax.ShapeDtypeStruct((STRIPES, ROWS, QP...  15.2 us
    unnamed x5, local copies, waits for them, and re-layouts  1.84 us

profile of v6, /device:TPU:0, one launch (start us, length us, event | category | flops | bytes accessed | tf_op | source)
XLA Modules:
  0.0 78.4 jit_solution(16109888601696156437)
XLA Ops:
  0.6 0.9 %add_bitcast_fusion.given = s32[128,128]{1,0:T(8,128)S(1)} fusion(s32[1024]{0:T(1024)} %param.11, s32[16384]{0:T(1024)} %param.9, s32[16384]{0:T(1024)} %param.10), kind=kLoop, calls=%fused_computation | loop fusion | flops 81920 | bytes 200704 | tf_op jit(solution)/shard_map/reshape | solution.py:532
  1.5 0.0 copy-start.1
  1.5 1.0 %copy-done.1 = bf16[128,2048]{1,0:T(8,128)(2,1)S(1)} copy-done((bf16[128,2048]{1,0:T(8,128)(2,1)S(1)}, bf16[128,2048]{1,0:T(8,128)(2,1)}, u32[]{:S(2)}) %copy-start.1) | copy-done | bytes 524312
  2.6 40.9 %project.1 = (bf16[8,128,256]{2,1,0:T(8,128)(2,1)S(1)}, bf16[16384,128]{1,0:T(8,128)(2,1)S(1)}, bf16[17408,128]{1,0:T(8,128)(2,1)S(1)}, bf16[80,17408]{1,0:T(8,1...) custom-call(bf16[128,2048]{1,0:T(8,128)(2,1)S(1)} %copy-done.1, bf16[2048,3072]{1,0:T(8,128)(2,1)} %w.2, ...), custom_call_target="tpu_custom_call" | custom-call | tf_op jit(solution)/shard_map/project/pallas_call | solution.py:499
  43.5 0.0 copy-start
  43.5 15.2 %attend.1 = (bf16[8,128,256]{2,1,0:T(8,128)(2,1)S(1)}, bf16[1024,128]{1,0:T(8,128)(2,1)}) custom-call(s32[72,128]{1,0:T(8,128)S(1)} %get-tuple-element.10.meta_in, s32[128,128]{1,0:T(8,128)S(1)} %get-tuple-element.11.code, bf16[8,128,256]{2,1,0:T(8,128)(2,1)S(1)} %get-tuple-element.12.q, bf16[16384,128]{1,0:T(8,128)(2,1)S(1)} %get-tuple-element.13.kv, ...), custom_call_target="tpu_custom_call" | custom-call | tf_op jit(solution)/shard_map/attend/pallas_call | solution.py:534
  58.7 0.0 copy-done
  58.7 18.9 %mix.1 = bf16[128,2048]{1,0:T(8,128)(2,1)S(1)} custom-call(bf16[8,128,256]{2,1,0:T(8,128)(2,1)S(1)} %get-tuple-element.16.att, bf16[2048,2048]{1,0:T(8,128)(2,1)S(1)} %copy-done), custom_call_target="tpu_custom_call" | custom-call | tf_op jit(solution)/shard_map/mix/pallas_call | solution.py:558
  77.6 0.8 %copy.9 = bf16[128,2048]{1,0:T(8,128)(2,1)} copy(bf16[128,2048]{1,0:T(8,128)(2,1)S(1)} %mix.1) | data formatting | bytes 1048576
Async XLA Ops:
  1.5 1.0 %copy-start.1 = (bf16[128,2048]{1,0:T(8,128)(2,1)S(1)}, bf16[128,2048]{1,0:T(8,128)(2,1)}, u32[]{:S(2)}) copy-start(bf16[128,2048]{1,0:T(8,128)(2,1)} %hv.1) | copy-start | bytes 1572868
  43.5 15.2 %copy-start = (bf16[2048,2048]{1,0:T(8,128)(2,1)S(1)}, bf16[2048,2048]{1,0:T(8,128)(2,1)}, u32[]{:S(2)}) copy-start(bf16[2048,2048]{1,0:T(8,128)(2,1)} %w.3) | copy-start | bytes 25165828

commit v7 on v6

--- a/solution.py
+++ b/solution.py
@@ -25,7 +25,7 @@
 META = STRIPES + 64
 CHUNKS = 2
 CH = GT // CHUNKS
-EARLY = 4
+FIRST = 3
 NEG = -1e30
 MESH = pl.DeviceIdType.MESH
 bf16, f32 = jnp.bfloat16, jnp.float32
@@ -88,7 +88,6 @@
         g = lax.rem(j + r + 1, 8)
         col = pl.multiple_of(g * COLS, 128)
         loads.append(pltpu.make_async_copy(w.at[:, pl.ds(col, QPK * HD)], wq.at[r], load.at[8 + r]))
-        loads[-1].start()
 
     def block(zz, xx, cc):
         return zz * 8 + xx * 2 + cc
@@ -150,17 +149,10 @@
         loads[8 + r].wait()
         qs[r] = (jnp.dot(hv[...], wq[r], preferred_element_type=f32).astype(bf16) * 0.015625).astype(bf16)
 
-    for r in range(8):
-        loads[r].wait()
-        kvs[r] = jnp.dot(hv[...], wk[r], preferred_element_type=f32).astype(bf16)
-    for r in range(EARLY):
-        query(r)
     row0 = pl.multiple_of(s * GT + j * ROWS, ROWS)
-    own_kv = pltpu.make_async_copy(kvs.at[7], kv_out.at[pl.ds(row0, ROWS)], loc)
-    own_kv.start()
-    pl.semaphore_wait(barrier, jnp.where(mine, 18, 19))
     sends = []
-    for r in range(7):
+
+    def send_keys(r):
         cp = pltpu.make_async_remote_copy(
             src_ref=kvs.at[r],
             dst_ref=kv_out.at[pl.ds(row0, ROWS)],
@@ -171,6 +163,21 @@
         )
         cp.start()
         sends.append(cp)
+
+    for r in range(8):
+        loads[r].wait()
+        if r == FIRST:
+            for n in range(8):
+                loads[8 + n].start()
+        kvs[r] = jnp.dot(hv[...], wk[r], preferred_element_type=f32).astype(bf16)
+        if r == FIRST:
+            pl.semaphore_wait(barrier, jnp.where(mine, 18, 19))
+            for n in range(r + 1):
+                send_keys(n)
+        elif FIRST < r < 7:
+            send_keys(r)
+    own_kv = pltpu.make_async_copy(kvs.at[7], kv_out.at[pl.ds(row0, ROWS)], loc)
+    own_kv.start()
 
     R, L, Z, C = range(4)
     held_at = {}
@@ -224,8 +231,7 @@
                 pltpu.make_async_copy(qs.at[7], q_out.at[slot], q_r.at[slot]).start()
 
     for r in range(8):
-        if r >= EARLY:
-            query(r)
+        query(r)
         send_query(r)
     tables()
     own_kv.wait()
@@ -303,18 +309,18 @@
             other("of", h - CHUNKS // 2, h)
             ready("zl", h - CHUNKS // 2)
             ready("zr", h - CHUNKS // 2)
+    ready("zl", *high)
+    ready("zr", *high)
     for h, g in zip(low, high, strict=True):
         arrived("zf", h, "of", Z)
         pass_on("zf", h, C)
-        ready("zl", g)
+        other("zl", h)
+        other("zr", h)
         arrived("zf", g, "of", Z)
         pass_on("zf", g, C)
-        ready("zr", g)
-        other("zl", h)
-        other("zr", h)
-    ready("zf", *low, *high)
     other("zl", *high)
     other("zr", *high)
+    ready("zf", *low, *high)
     other("zf", *low, *high)
 
     for k in range(STRIPES):
@@ -447,7 +453,8 @@
     pl.semaphore_wait(barrier, jnp.where(mine, 7, 8))
 
     copies = []
-    for k in range(STRIPES):
+    for r in range(STRIPES):
+        k = lax.rem(s // 2 + j + r, STRIPES)
         own = mine & (s // 2 == k)
         cp = pltpu.make_async_remote_copy(
             src_ref=att.at[k],

time: 79.7 us -> 84.9 us (1.065); the launches traced: 78.4 us -> 84.7 us
  Pallas kernels: 75 us -> 81.2 us
    pallas_call x1, Pallas kernels: 18.9 us -> 25.4 us  [shards(): pl.pallas_call(mix, out_shape=jax.ShapeDtypeStruct((ROWS, D), bf16), in_s...]
    pallas_call x1, Pallas kernels: 40.9 us -> 37.6 us  [projected(): pl.pallas_call(project, out_shape=(jax.ShapeDtypeStruct((STRIPES, ROWS, Q...]
    pallas_call x1, Pallas kernels: 15.2 us -> 18.3 us  [shards(): pl.pallas_call(attend, out_shape=(jax.ShapeDtypeStruct((STRIPES, ROWS, QP...]
where the time goes in v7:
time: 84.9 us; the launch traced here: 84.7 us
  Pallas kernels  81.2 us (96%)
  local copies, waits for them, and re-layouts  1.84 us (2%)
  other arithmetic  0.9 us (1%)
    pallas_call x1, Pallas kernels, projected(): pl.pallas_call(project, out_shape=(jax.ShapeDtypeStruct((STRIPES, ROWS, Q...  37.6 us
    pallas_call x1, Pallas kernels, shards(): pl.pallas_call(mix, out_shape=jax.ShapeDtypeStruct((ROWS, D), bf16), in_s...  25.4 us
    pallas_call x1, Pallas kernels, shards(): pl.pallas_call(attend, out_shape=(jax.ShapeDtypeStruct((STRIPES, ROWS, QP...  18.3 us
    unnamed x5, local copies, waits for them, and re-layouts  1.84 us

profile of v7, /device:TPU:0, one launch (start us, length us, event | category | flops | bytes accessed | tf_op | source)
XLA Modules:
  0.0 84.7 jit_solution(9598905245905424430)
XLA Ops:
  0.6 0.9 %add_bitcast_fusion.given = s32[128,128]{1,0:T(8,128)S(1)} fusion(s32[1024]{0:T(1024)} %param.11, s32[16384]{0:T(1024)} %param.9, s32[16384]{0:T(1024)} %param.10), kind=kLoop, calls=%fused_computation | loop fusion | flops 81920 | bytes 200704 | tf_op jit(solution)/shard_map/reshape | solution.py:539
  1.5 0.0 copy-start.1
  1.5 1.0 %copy-done.1 = bf16[128,2048]{1,0:T(8,128)(2,1)S(1)} copy-done((bf16[128,2048]{1,0:T(8,128)(2,1)S(1)}, bf16[128,2048]{1,0:T(8,128)(2,1)}, u32[]{:S(2)}) %copy-start.1) | copy-done | bytes 524312
  2.6 37.6 %project.1 = (bf16[8,128,256]{2,1,0:T(8,128)(2,1)S(1)}, bf16[16384,128]{1,0:T(8,128)(2,1)S(1)}, bf16[17408,128]{1,0:T(8,128)(2,1)S(1)}, bf16[80,17408]{1,0:T(8,1...) custom-call(bf16[128,2048]{1,0:T(8,128)(2,1)S(1)} %copy-done.1, bf16[2048,3072]{1,0:T(8,128)(2,1)} %w.2, ...), custom_call_target="tpu_custom_call" | custom-call | tf_op jit(solution)/shard_map/project/pallas_call | solution.py:506
  40.2 0.0 copy-start
  40.2 18.3 %attend.1 = (bf16[8,128,256]{2,1,0:T(8,128)(2,1)S(1)}, bf16[1024,128]{1,0:T(8,128)(2,1)}) custom-call(s32[72,128]{1,0:T(8,128)S(1)} %get-tuple-element.10.meta_in, s32[128,128]{1,0:T(8,128)S(1)} %get-tuple-element.11.code, bf16[8,128,256]{2,1,0:T(8,128)(2,1)S(1)} %get-tuple-element.12.q, bf16[16384,128]{1,0:T(8,128)(2,1)S(1)} %get-tuple-element.13.kv, ...), custom_call_target="tpu_custom_call" | custom-call | tf_op jit(solution)/shard_map/attend/pallas_call | solution.py:541
  58.4 0.0 copy-done
  58.5 25.4 %mix.1 = bf16[128,2048]{1,0:T(8,128)(2,1)S(1)} custom-call(bf16[8,128,256]{2,1,0:T(8,128)(2,1)S(1)} %get-tuple-element.16.att, bf16[2048,2048]{1,0:T(8,128)(2,1)S(1)} %copy-done), custom_call_target="tpu_custom_call" | custom-call | tf_op jit(solution)/shard_map/mix/pallas_call | solution.py:565
  83.9 0.8 copy.9
Async XLA Ops:
  1.5 1.0 %copy-start.1 = (bf16[128,2048]{1,0:T(8,128)(2,1)S(1)}, bf16[128,2048]{1,0:T(8,128)(2,1)}, u32[]{:S(2)}) copy-start(bf16[128,2048]{1,0:T(8,128)(2,1)} %hv.1) | copy-start | bytes 1572868
  40.2 18.3 %copy-start = (bf16[2048,2048]{1,0:T(8,128)(2,1)S(1)}, bf16[2048,2048]{1,0:T(8,128)(2,1)}, u32[]{:S(2)}) copy-start(bf16[2048,2048]{1,0:T(8,128)(2,1)} %w.3) | copy-start | bytes 25165828

commit v8 on v7

--- a/solution.py
+++ b/solution.py
@@ -19,7 +19,7 @@
 GT = 1024
 COLS = (QPK + 2) * HD
 STRIPES = 8
-BK = 512
+BK = 640
 PAD = 2 * BK
 ITEMS = STRIPES * (TOKENS // BK) + 8
 META = STRIPES + 64
@@ -123,7 +123,8 @@
             own = code[pl.ds(stripe, 1), :][:, :1] & 15
             before = jnp.where(seg < own, 1.0, 0.0)
             begin = jnp.sum(jnp.sum(before, axis=0, keepdims=True), axis=1, keepdims=True).astype(jnp.int32)
-            blocks = lax.shift_right_logical(stripe * ROWS - begin + BK - 1, BK.bit_length() - 1)
+            blocks = ((stripe * ROWS - begin + BK - 1).astype(f32) + 0.5) * (1.0 / BK)
+            blocks = blocks.astype(jnp.int32)
             meta[k : k + 1, :] = jnp.where(lane == 0, blocks, own)
         at = jnp.zeros((64, 128), f32)
         for n in range(TOKENS // PAGE // 128):

time: 84.9 us -> 78 us (0.919)
  Pallas kernels: 81.2 us -> 75 us
    pallas_call x1, Pallas kernels: 25.4 us -> 16.9 us  [shards(): pl.pallas_call(mix, out_shape=jax.ShapeDtypeStruct((ROWS, D), bf16), in_s...]
    pallas_call x1, Pallas kernels: 18.3 us -> 20.5 us  [shards(): pl.pallas_call(attend, out_shape=(jax.ShapeDtypeStruct((STRIPES, ROWS, QP...]
where the time goes in v8:
time: 78 us; the launch traced here: 78.4 us
  Pallas kernels  75 us (96%)
  local copies, waits for them, and re-layouts  1.84 us (2%)
  other arithmetic  0.9 us (1%)
    pallas_call x1, Pallas kernels, projected(): pl.pallas_call(project, out_shape=(jax.ShapeDtypeStruct((STRIPES, ROWS, Q...  37.6 us
    pallas_call x1, Pallas kernels, shards(): pl.pallas_call(attend, out_shape=(jax.ShapeDtypeStruct((STRIPES, ROWS, QP...  20.5 us
    pallas_call x1, Pallas kernels, shards(): pl.pallas_call(mix, out_shape=jax.ShapeDtypeStruct((ROWS, D), bf16), in_s...  16.9 us
    unnamed x5, local copies, waits for them, and re-layouts  1.84 us

profile of v8, /device:TPU:0, one launch (start us, length us, event | category | flops | bytes accessed | tf_op | source)
XLA Modules:
  0.0 78.4 jit_solution(4071113661742191526)
XLA Ops:
  0.6 0.9 %add_bitcast_fusion.given = s32[128,128]{1,0:T(8,128)S(1)} fusion(s32[1024]{0:T(1024)} %param.11, s32[16384]{0:T(1024)} %param.9, s32[16384]{0:T(1024)} %param.10), kind=kLoop, calls=%fused_computation | loop fusion | flops 81920 | bytes 200704 | tf_op jit(solution)/shard_map/reshape | solution.py:540
  1.5 0.0 copy-start.1
  1.5 1.0 %copy-done.1 = bf16[128,2048]{1,0:T(8,128)(2,1)S(1)} copy-done((bf16[128,2048]{1,0:T(8,128)(2,1)S(1)}, bf16[128,2048]{1,0:T(8,128)(2,1)}, u32[]{:S(2)}) %copy-start.1) | copy-done | bytes 524312
  2.6 37.6 %project.1 = (bf16[8,128,256]{2,1,0:T(8,128)(2,1)S(1)}, bf16[16384,128]{1,0:T(8,128)(2,1)S(1)}, bf16[17664,128]{1,0:T(8,128)(2,1)S(1)}, bf16[80,17664]{1,0:T(8,1...) custom-call(bf16[128,2048]{1,0:T(8,128)(2,1)S(1)} %copy-done.1, bf16[2048,3072]{1,0:T(8,128)(2,1)} %w.2, ...), custom_call_target="tpu_custom_call" | custom-call | tf_op jit(solution)/shard_map/project/pallas_call | solution.py:507
  40.2 0.0 copy-start
  40.2 20.5 %attend.1 = (bf16[8,128,256]{2,1,0:T(8,128)(2,1)S(1)}, bf16[1024,128]{1,0:T(8,128)(2,1)}) custom-call(s32[72,128]{1,0:T(8,128)S(1)} %get-tuple-element.10.meta_in, s32[128,128]{1,0:T(8,128)S(1)} %get-tuple-element.11.code, bf16[8,128,256]{2,1,0:T(8,128)(2,1)S(1)} %get-tuple-element.12.q, bf16[16384,128]{1,0:T(8,128)(2,1)S(1)} %get-tuple-element.13.kv, ...), custom_call_target="tpu_custom_call" | custom-call | tf_op jit(solution)/shard_map/attend/pallas_call | solution.py:542
  60.7 0.0 copy-done
  60.7 16.9 %mix.1 = bf16[128,2048]{1,0:T(8,128)(2,1)S(1)} custom-call(bf16[8,128,256]{2,1,0:T(8,128)(2,1)S(1)} %get-tuple-element.16.att, bf16[2048,2048]{1,0:T(8,128)(2,1)S(1)} %copy-done), custom_call_target="tpu_custom_call" | custom-call | tf_op jit(solution)/shard_map/mix/pallas_call | solution.py:566
  77.6 0.8 %copy.9 = bf16[128,2048]{1,0:T(8,128)(2,1)} copy(bf16[128,2048]{1,0:T(8,128)(2,1)S(1)} %mix.1) | data formatting | bytes 1048576
Async XLA Ops:
  1.5 1.0 %copy-start.1 = (bf16[128,2048]{1,0:T(8,128)(2,1)S(1)}, bf16[128,2048]{1,0:T(8,128)(2,1)}, u32[]{:S(2)}) copy-start(bf16[128,2048]{1,0:T(8,128)(2,1)} %hv.1) | copy-start | bytes 1572868
  40.2 20.6 %copy-start = (bf16[2048,2048]{1,0:T(8,128)(2,1)S(1)}, bf16[2048,2048]{1,0:T(8,128)(2,1)}, u32[]{:S(2)}) copy-start(bf16[2048,2048]{1,0:T(8,128)(2,1)} %w.3) | copy-start | bytes 25165828
